TPU v7x, 512 devices: a whole 4x4x16 slice. The times are simulated.
512 devices in a mesh: section: 4 (over x), bins: 128 (over y, z, core).
Axes of the slice: x: 4, y: 4, z: 16, core: 2. Of those that a mesh axis runs over, the one named last changes fastest.
Arguments:
- traces: float32 [8192, 4096], P('bins', 'section'), may hold values from -6 to 6
- filters: float32 [128, 256], P('bins'), may hold values from -0.375 to 0.375
- owners: int32 [8192, 1], P('bins'), may hold values from 0 to 127; in each aligned block of 64 rows (0 to 63, 64 to 127, ...) at most 2 rows name the same one
- sub_bins: int32 [8192], P('bins'), may hold values from 0 to 7
- sample_map: int32 [8192, 4096], P('bins', 'section'), may hold values from 0 to 1019
Outputs:
- stack: float32 [1024, 4096], P('bins', 'section')
Inputs may be any that keep to these rules, and one draw needn't show every extreme that they name: `owners`: in each aligned block of 64 rows (the traces of one shot) no owner is named more than 2 times; in some block one owner is named exactly 2 times.
All inputs are finite; a program needn't handle non-finite values.
Results may differ from a plain program's by a relative error of at most 0.0003.
Values sent between devices are 32-bit elements; how exact they have to be, the bound alone decides.
No kernel may reach another device: no remote copies, remote signals or barrier semaphores. Data moves between devices by JAX's collectives and lax.ppermute only.
A program may use at most 64 MiB of HBM per device.

v0:
```python
import jax
import jax.numpy as jnp
from jax import lax
from jax.sharding import PartitionSpec as P

BIN_DEV = 8


def passed_along(value, axis, steps):
    count = lax.axis_size(axis)
    leading, last = (max(0, -steps), min(count, count - steps))
    return lax.ppermute(value, axis, [(source, source + steps) for source in range(leading, last)])


def toeplitz_pair(filt):
    taps = filt.shape[0]
    zeros = jnp.zeros((taps,), filt.dtype)
    padded = jnp.concatenate([zeros, filt, zeros])
    starts = jnp.arange(taps, dtype=jnp.int32)

    def lower_row(j):
        return lax.dynamic_slice_in_dim(padded, taps - j, taps)

    def upper_row(j):
        return lax.dynamic_slice_in_dim(padded, 2 * taps - j, taps)

    return (jax.vmap(lower_row)(starts), jax.vmap(upper_row)(starts))


def deconvolve(current, previous, lower, upper):
    first = jnp.einsum("rbj,ji->rbi", current, lower, precision=lax.Precision.HIGHEST)
    second = jnp.einsum("rbj,ji->rbi", previous, upper, precision=lax.Precision.HIGHEST)
    return first + second


def move_out(window, quarter, anchor):
    rows, span = window.shape
    whole = quarter // 4 - anchor
    weight = (quarter % 4).astype(jnp.float32) * 0.25
    row_base = (jnp.arange(rows, dtype=jnp.int32) * span)[:, None]
    flat_index = (whole + row_base).reshape(-1)
    both_index = jnp.concatenate([flat_index, flat_index + 1])
    picked = jnp.take(window.reshape(-1), both_index, axis=0)
    count = flat_index.shape[0]
    near = picked[:count].reshape(quarter.shape)
    far = picked[count:].reshape(quarter.shape)
    return near + weight * (far - near)


def per_device(traces, filters, owners, sub_bins, sample_map):
    rows, width = traces.shape
    taps = filters.shape[1]
    lower, upper = toeplitz_pair(filters[0])
    blocks = traces.reshape(rows, width // taps, taps)
    place = lax.axis_index("section")
    before = passed_along(traces[:, width - taps :], "section", 1)
    previous = jnp.concatenate([before[:, None, :], blocks[:, :-1]], axis=1)
    deconvolved = deconvolve(blocks, previous, lower, upper).reshape(rows, width)
    tail = passed_along(deconvolved[:, :taps], "section", -1)
    window = jnp.concatenate([deconvolved, tail], axis=1)
    times = 4 * (place * width + jnp.arange(width, dtype=jnp.int32))
    quarter = sample_map + times[None, :]
    corrected = move_out(window, quarter, place * width)
    owner_count = lax.axis_size("bins")
    owner = owners[:, 0]
    capacity = max(2, 2 * rows // owner_count)
    columns = jnp.arange(owner_count, dtype=jnp.int32)
    onehot = (owner[:, None] == columns[None, :]).astype(jnp.int32)
    rank = jnp.sum((jnp.cumsum(onehot, axis=0) - 1) * onehot, axis=1)
    slots = jnp.zeros((owner_count, capacity, width), jnp.float32).at[owner, rank].set(corrected)
    labels = (
        jnp.zeros((owner_count, capacity), jnp.float32)
        .at[owner, rank]
        .set((sub_bins + 1).astype(jnp.float32))
    )
    arrived, arrived_labels = (
        lax.all_to_all(slots, "bins", split_axis=0, concat_axis=0, tiled=True),
        lax.all_to_all(labels, "bins", split_axis=0, concat_axis=0, tiled=True),
    )
    flat_slots = arrived.reshape(owner_count * capacity, width)
    flat_labels = arrived_labels.reshape(owner_count * capacity)
    targets = (jnp.arange(BIN_DEV, dtype=jnp.int32) + 1).astype(jnp.float32)
    member = (flat_labels[None, :] == targets[:, None]).astype(jnp.float32)
    summed = jnp.dot(
        member, flat_slots, precision=lax.Precision.HIGHEST, preferred_element_type=jnp.float32
    )
    counts = jnp.sum(member, axis=1)
    scale = jnp.sqrt(jnp.maximum(counts, 1.0))
    return summed / scale[:, None]


def solution(mesh):
    in_specs = (
        P("bins", "section"),
        P("bins", None),
        P("bins", None),
        P("bins"),
        P("bins", "section"),
    )
    out_specs = P("bins", "section")
    return jax.shard_map(
        per_device, mesh=mesh, in_specs=in_specs, out_specs=out_specs, check_vma=False
    )
```

profile of v0, /device:TPU:6, one launch (start us, length us, event | category | flops | bytes accessed | tf_op | source)
XLA Modules:
  0.0 1541.5 jit_solution(1221875392746745904)
XLA Ops:
  0.0 0.8 slice.17
  0.8 1.4 collective-permute-start
  3.9 3.5 scatter_fusion
  7.3 0.7 copy.14
  8.1 20.5 %all-to-all-start = ((f32[128,1,2]{2,1,0:T(1,128)}), f32[128,1,2]{2,1,0:T(1,128)}, u32[]{:S(2)}, u32[]{:S(2)}) async-start(f32[128,1,2]{2,1,0:T(1,128)} %copy.14), calls=%async_computation | async-start | bytes 131072 | tf_op jit(solution)/shard_map/all_to_all | solution.py:78
  28.7 0.9 broadcast_add_fusion
  31.6 351.4 %while.2 = (s32[]{:T(128)}, f32[768]{0:T(1024)S(1)}, s32[256,1]{0,1:T(1,128)S(1)}, f32[256,256]{1,0:T(8,128)S(1)}, s32[]{:T(128)}, /*index=5*/s32[]{:T(128)}) while((s32[]{:T(128)}, f32[768]{0:T(1024)S(1)}, s32[256,1]{0,1:T(1,128)S(1)}, f32[256,256]{1,0:T(8,128)S(1)}, s32[]{:T(128)}, /*index=5*/s32[]{:T(128)}) %tuple.28), condition=%wide.while_cond, body=%wide.while_body.sunk | while | flops 2 | bytes 4185 | solution.py:22
  383.4 340.3 %while.3 = (s32[]{:T(128)}, f32[768]{0:T(1024)S(1)}, s32[256,1]{0,1:T(1,128)S(1)}, f32[256,256]{1,0:T(8,128)S(1)}, s32[]{:T(128)}, /*index=5*/s32[]{:T(128)}) while((s32[]{:T(128)}, f32[768]{0:T(1024)S(1)}, s32[256,1]{0,1:T(1,128)S(1)}, f32[256,256]{1,0:T(8,128)S(1)}, s32[]{:T(128)}, /*index=5*/s32[]{:T(128)}) %tuple.34), condition=%wide.while_cond.1, body=%wide.while_body.1.sunk | while | flops 2 | bytes 4185 | solution.py:25
  384.0 0.7 dynamic-slice.15
  385.4 0.7 dynamic-slice.15
  388.0 0.7 dynamic-slice.15
  389.4 0.7 dynamic-slice.15
  392.0 0.7 dynamic-slice.15
  393.3 0.7 dynamic-slice.15
  396.0 0.7 dynamic-slice.15
  397.3 0.7 dynamic-slice.15
  401.3 0.7 dynamic-slice.15
  405.3 0.7 dynamic-slice.15
  409.3 0.7 dynamic-slice.15
  410.6 0.7 dynamic-slice.15
  724.3 4.5 collective-permute-start.1
  728.9 1.8 collective-permute-done.1
  730.8 724.9 %gather_fusion = f32[131072]{0:T(1024)S(1)} fusion(f32[81920]{0:T(1024)S(1)} %reshape.193, s32[131072]{0:T(1024)S(1)} %broadcast_clamp_fusion), kind=kCustom, calls=%fused_computation | custom fusion | bytes 1572864 | tf_op jit(solution)/shard_map/jit(_take)/gather | solution.py:43
  1455.8 0.8 copy-done.3
  1456.8 0.8 copy-done.6
  1457.8 1.2 broadcast_in_dim.15
  1459.1 8.8 scatter_fusion.1
  1467.9 16.1 %all-to-all-start.1 = ((f32[128,2,1024]{2,1,0:T(2,128)}), f32[128,2,1024]{2,1,0:T(2,128)S(1)}, u32[]{:S(2)}, u32[]{:S(2)}) async-start(f32[128,2,1024]{2,1,0:T(2,128)} %scatter_fusion.1), calls=%async_computation.1 | async-start | bytes 2097152 | tf_op jit(solution)/shard_map/all_to_all | solution.py:77
  1484.5 1.6 reduce.3
  1486.5 53.1 %all-to-all-done.1 = f32[128,2,1024]{2,1,0:T(2,128)S(1)} async-done(((f32[128,2,1024]{2,1,0:T(2,128)}), f32[128,2,1024]{2,1,0:T(2,128)S(1)}, u32[]{:S(2)}, u32[]{:S(2)}) %all-to-all-start.1) | async-done | bytes 1048608 | tf_op jit(solution)/shard_map/all_to_all | solution.py:77
  1539.6 0.7 reshape.194
  1540.4 1.1 convolution_divide_fusion
  (1587 shorter events, 681.7 us)
Async XLA Ops:
  0.8 1.4 copy-start.10
  0.8 723.0 %collective-permute-start = (f32[64,256]{1,0:T(8,128)S(1)}, f32[64,256]{1,0:T(8,128)S(1)}, u32[]{:S(2)}, u32[]{:S(2)}) collective-permute-start(f32[64,256]{1,0:T(8,128)S(1)} %slice.17), channel_id=1, source_target_pairs={{0,128},{128,256},{256,384},{1,129},{129,257},{257,385},{2,130},{1... | collective-permute-start | bytes 196616 | tf_op jit(solution)/shard_map/ppermute | solution.py:12
  2.6 0.7 copy-start.12
  3.3 0.6 copy-start
  3.9 24.8 %copy-start.5 = (s32[64,1024]{1,0:T(8,128)S(1)}, s32[64,1024]{1,0:T(8,128)}, u32[]{:S(2)}) copy-start(s32[64,1024]{1,0:T(8,128)} %param.9) | copy-start | bytes 786436
  8.1 1459.8 %all-to-all-start = ((f32[128,1,2]{2,1,0:T(1,128)}), f32[128,1,2]{2,1,0:T(1,128)}, u32[]{:S(2)}, u32[]{:S(2)}) async-start(f32[128,1,2]{2,1,0:T(1,128)} %copy.14), calls=%async_computation | async-start | bytes 131072 | tf_op jit(solution)/shard_map/all_to_all | solution.py:78
  28.6 0.9 copy-start.8
  29.6 0.7 copy-start.2
  30.9 0.7 copy-start.11
  31.4 351.6 %copy-start.4 = (f32[64,1024]{1,0:T(8,128)S(1)}, f32[64,1024]{1,0:T(8,128)}, u32[]{:S(2)}) copy-start(f32[64,1024]{1,0:T(8,128)} %param.5) | copy-start | bytes 786436
  724.3 6.4 collective-permute-start.1
  1455.7 1.0 copy-start.3
  1455.7 1.0 copy-start.7
  1456.7 0.9 copy-start.6
  1456.7 1.0 copy-start.9
  1457.8 1.3 copy-start.1
  1467.9 71.8 %all-to-all-start.1 = ((f32[128,2,1024]{2,1,0:T(2,128)}), f32[128,2,1024]{2,1,0:T(2,128)S(1)}, u32[]{:S(2)}, u32[]{:S(2)}) async-start(f32[128,2,1024]{2,1,0:T(2,128)} %scatter_fusion.1), calls=%async_computation.1 | async-start | bytes 2097152 | tf_op jit(solution)/shard_map/all_to_all | solution.py:77
where the time goes:
time: 1550 us; the launch traced here: 1540 us
  local copies, waits for them, and re-layouts  1430 us (92%)
  waiting for transfers between devices  55 us (4%)
  starting transfers between devices  42.6 us (3%)
    gather x2, local copies, waits for them, and re-layouts, move_out(): picked = jnp.take(window.reshape(-1), both_index, axis=0)  725 us
    gather x1536, local copies, waits for them, and re-layouts  684 us
    all_to_all x1, waiting for transfers between devices, per_device(): lax.all_to_all(slots, 'bins', split_axis=0, concat_axis=0, tiled=True)  53.1 us
  transfers between devices with their start and end apart: 4, of which 2 were waited for; matrix products, arithmetic and copies ran while one was open for 93% of the time, Pallas kernels for 0%

commit v1 on v0

v1 whole, which is shorter than its diff:
```python
import functools

import jax
import jax.numpy as jnp
import numpy as np
from jax import lax
from jax.experimental import pallas as pl
from jax.experimental.pallas import tpu as pltpu
from jax.sharding import Mesh
from jax.sharding import PartitionSpec as P

BIN_DEV = 8
LANES = 128
NY, NZ, NC = 4, 16, 2
BINS = ("y", "z", "c")


def halves(value):
    high = value.astype(jnp.bfloat16)
    low = (value - high.astype(jnp.float32)).astype(jnp.bfloat16)
    return high, low


def dot(a, b):
    return jnp.dot(a, b, preferred_element_type=jnp.float32)


def correct_kernel(last_ref, traces_ref, before_ref, after_ref, filter_ref, label_ref, map_ref, out_ref):
    rows, width = traces_ref.shape
    taps = filter_ref.shape[1]
    count = width // taps
    padded = jnp.concatenate([filter_ref[...], jnp.zeros((1, taps), jnp.float32)], axis=1)
    shifted = pltpu.roll(jnp.broadcast_to(padded, (taps, 2 * taps)), 0, 1, stride=1, stride_axis=0)
    toeplitz_high, toeplitz_low = halves(shifted)
    blocks = [before_ref[...]]
    blocks += [traces_ref[:, b * taps : (b + 1) * taps] for b in range(count)]
    blocks += [after_ref[...]]
    stacked_high, stacked_low = halves(jnp.concatenate(blocks, axis=0))
    spread = dot(stacked_high, toeplitz_high) + (dot(stacked_low, toeplitz_high) + dot(stacked_high, toeplitz_low))
    pieces = []
    for b in range(1, count + 2):
        piece = spread[b * rows : (b + 1) * rows, :taps] + spread[(b - 1) * rows : b * rows, taps:]
        if b == count + 1:
            piece = jnp.where(last_ref[0] == 1, 0.0, piece)
        pieces.append(piece)
    window = jnp.concatenate(pieces, axis=1)
    span = window.shape[1]
    step = pltpu.roll(window, span - 1, 1) - window
    lane = lax.broadcasted_iota(jnp.int32, (rows, LANES), 1)
    for c in range(width // LANES):
        quarter = map_ref[:, c * LANES : (c + 1) * LANES]
        place = lane + (quarter >> 2)
        weight = (quarter & 3).astype(jnp.float32) * 0.25
        inside = place & (LANES - 1)
        block = place >> 7
        near = far = None
        for k in range(3):
            columns = slice((c + k) * LANES, (c + k + 1) * LANES)
            value = jnp.take_along_axis(window[:, columns], inside, axis=1, mode="promise_in_bounds")
            slope = jnp.take_along_axis(step[:, columns], inside, axis=1, mode="promise_in_bounds")
            near = value if k == 0 else jnp.where(block == k, value, near)
            far = slope if k == 0 else jnp.where(block == k, slope, far)
        moved = near + weight * far
        for y in range(NY):
            out_ref[y, c * rows : (c + 1) * rows, :] = moved
    for y in range(NY):
        out_ref[y, width // LANES * rows :, :] = label_ref[...]


def combine_kernel(first_ref, arrived_ref, *refs):
    out_ref = refs[-1]
    parts = out_ref.shape[1] // BIN_DEV - 1
    rows = (arrived_ref.shape[1] - BIN_DEV) // parts
    tile = arrived_ref[0, parts * rows :, :]
    for y in range(1, NY):
        tile = tile + arrived_ref[y, parts * rows :, :]
    labels = jnp.concatenate([tile[0:1, :], tile[1:2, :]], axis=1)
    row = lax.broadcasted_iota(jnp.int32, (NZ * BIN_DEV, 1), 0)
    number = first_ref[0] + (row // BIN_DEV) * (NC * BIN_DEV) + row % BIN_DEV
    hit = labels == number.astype(jnp.float32)
    member = jnp.where(hit, 1.0, 0.0).astype(jnp.bfloat16)
    for c in range(parts):
        piece = jnp.concatenate([arrived_ref[y, c * rows : (c + 1) * rows, :] for y in range(NY)], axis=0)
        high, low = halves(piece)
        total = (dot(member, high) + dot(member, low)).reshape(NZ, BIN_DEV, LANES)
        if len(refs) == 2:
            total = total + refs[0][:, c * BIN_DEV : (c + 1) * BIN_DEV, :]
        out_ref[:, c * BIN_DEV : (c + 1) * BIN_DEV, :] = total
    fold = dot(member, jnp.ones((NY * rows, LANES), jnp.bfloat16)).reshape(NZ, BIN_DEV, LANES)
    if len(refs) == 2:
        fold = fold + refs[0][:, parts * BIN_DEV :, :]
    out_ref[:, parts * BIN_DEV :, :] = fold


def finish_kernel(arrived_ref, out_ref):
    total = arrived_ref[0]
    for z in range(1, NZ):
        total = total + arrived_ref[z]
    parts = total.shape[0] // BIN_DEV - 1
    scale = jnp.sqrt(jnp.maximum(total[parts * BIN_DEV :, :], 1.0))
    for c in range(parts):
        out_ref[:, c * LANES : (c + 1) * LANES] = total[c * BIN_DEV : (c + 1) * BIN_DEV, :] / scale


VMEM = pl.BlockSpec(memory_space=pltpu.VMEM)
SMEM = pl.BlockSpec(memory_space=pltpu.SMEM)


def call(kernel, shape, name, *operands):
    specs = [SMEM if operand.dtype == jnp.int32 and operand.ndim == 1 else VMEM for operand in operands]
    return pl.pallas_call(
        kernel,
        out_shape=jax.ShapeDtypeStruct(shape, jnp.float32),
        in_specs=specs,
        out_specs=VMEM,
        name=name,
        compiler_params=pltpu.CompilerParams(vmem_limit_bytes=40 * 1024 * 1024),
    )(*operands)


def passed_along(value, axis, steps):
    count = lax.axis_size(axis)
    leading, last = (max(0, -steps), min(count, count - steps))
    return lax.ppermute(value, axis, [(source, source + steps) for source in range(leading, last)])


def per_device(traces, filters, owners, sub_bins, sample_map):
    rows, width = traces.shape
    taps = filters.shape[1]
    parts = width // LANES
    before = passed_along(traces[:, width - taps :], "section", 1)
    after = passed_along(traces[:, :taps], "section", -1)
    y, c = lax.axis_index("y"), lax.axis_index("c")
    last = (lax.axis_index("section") == lax.axis_size("section") - 1).astype(jnp.int32).reshape(1)
    label = (owners[:, 0] * BIN_DEV + sub_bins).astype(jnp.float32)
    tile = lax.dynamic_update_slice(jnp.zeros((BIN_DEV, LANES), jnp.float32), label[None, :], (y // 2, (y % 2) * rows))
    sent = call(
        correct_kernel, (NY, parts * rows + BIN_DEV, LANES), "correct",
        last, traces, before, after, filters, tile, sample_map,
    )
    gathered = lax.all_to_all(sent, "y", split_axis=0, concat_axis=0, tiled=True)
    shape = (NZ, (parts + 1) * BIN_DEV, LANES)

    def first(core):
        return ((y * NZ * NC + core) * BIN_DEV).astype(jnp.int32).reshape(1)

    other = call(combine_kernel, shape, "combine_other", first(1 - c), gathered)
    other = lax.ppermute(other, "c", [(0, 1), (1, 0)])
    summed = call(combine_kernel, shape, "combine_own", first(c), gathered, other)
    arrived = lax.all_to_all(summed, "z", split_axis=0, concat_axis=0, tiled=True)
    return call(finish_kernel, (BIN_DEV, width), "finish", arrived)


def solution(mesh):
    fine = Mesh(mesh.devices.reshape(mesh.devices.shape[0], NY, NZ, NC), ("section",) + BINS)
    in_specs = (
        P(BINS, "section"),
        P(BINS, None),
        P(BINS, None),
        P(BINS),
        P(BINS, "section"),
    )
    return jax.shard_map(
        per_device, mesh=fine, in_specs=in_specs, out_specs=P(BINS, "section"), check_vma=False
    )
```

time: 1550 us -> 89.4 us (0.06)
  local copies, waits for them, and re-layouts: 1430 us -> 3.58 us
  blocking collectives: 0 us -> 50.1 us
  waiting for transfers between devices: 55 us -> 19.8 us
  starting transfers between devices: 42.6 us -> 10.4 us
    gather x1538 -> x0, local copies, waits for them, and re-layouts: 1410 us -> none  [the longest x2 725 us: move_out(): picked = jnp.take(window.reshape(-1), both_index, axis=0)]
    all_to_all x0 -> x1, blocking collectives: none -> 50.1 us  [per_device(): lax.all_to_all(summed, 'z', split_axis=0, concat_axis=0, tiled=True)]
    all_to_all x2 -> x1, waiting for transfers between devices: 53.1 us -> 13.8 us  [per_device(): lax.all_to_all(sent, 'y', split_axis=0, concat_axis=0, tiled=True)]
    all_to_all x2 -> x1, starting transfers between devices: 36.6 us -> 4.46 us  [per_device(): lax.all_to_all(sent, 'y', split_axis=0, concat_axis=0, tiled=True)]
  transfers between devices with their start and end apart: 4 -> 4, of which waited for: 2 -> 3; matrix products, arithmetic and copies ran while one was open for 93% -> 1% of each run, Pallas kernels for 0% -> 0%
where the time goes in v1:
time: 89.4 us; the launch traced here: 89 us
  blocking collectives  50.1 us (56%)
  waiting for transfers between devices  19.8 us (22%)
  starting transfers between devices  10.4 us (12%)
  Pallas kernels  4.27 us (5%)
  local copies, waits for them, and re-layouts  3.58 us (4%)
    all_to_all x1, blocking collectives, per_device(): lax.all_to_all(summed, 'z', split_axis=0, concat_axis=0, tiled=True)  50.1 us
    all_to_all x1, waiting for transfers between devices, per_device(): lax.all_to_all(sent, 'y', split_axis=0, concat_axis=0, tiled=True)  13.8 us
    all_to_all x1, starting transfers between devices, per_device(): lax.all_to_all(sent, 'y', split_axis=0, concat_axis=0, tiled=True)  4.46 us
    pallas_call x4, Pallas kernels, call(): pl.pallas_call(kernel, out_shape=jax.ShapeDtypeStruct(shape, jnp.float32)...  4.27 us
    ppermute x2, waiting for transfers between devices, passed_along(): lax.ppermute(value, axis, [(source, source + steps) for source in range(l...  4.04 us
    ppermute x2, starting transfers between devices, passed_along(): lax.ppermute(value, axis, [(source, source + steps) for source in range(l...  4.03 us
    unnamed x6, local copies, waits for them, and re-layouts  2.58 us
    ppermute x1, waiting for transfers between devices, per_device(): other = lax.ppermute(other, 'c', [(0, 1), (1, 0)])  1.96 us
  transfers between devices with their start and end apart: 4, of which 3 were waited for; matrix products, arithmetic and copies ran while one was open for 1% of the time, Pallas kernels for 0%

profile of v1, /device:TPU:6, one launch (start us, length us, event | category | flops | bytes accessed | tf_op | source)
XLA Modules:
  0.0 89.0 jit_solution(9973849270364849319)
XLA Ops:
  0.0 0.9 fusion.2
  0.9 2.7 %collective-permute-start.1 = (f32[64,256]{1,0:T(8,128)S(1)}, f32[64,256]{1,0:T(8,128)S(1)}, u32[]{:S(2)}, u32[]{:S(2)}) collective-permute-start(f32[64,256]{1,0:T(8,128)S(1)} %get-tuple-element.5), channel_id=1, source_target_pairs={{128,0},{256,128},{384,256},{129,1},{257,129},{385,257},{130,2},{2... | collective-permute-start | bytes 196616 | tf_op jit(solution)/shard_map/ppermute | solution.py:124
  3.6 1.3 %collective-permute-start = (f32[64,256]{1,0:T(8,128)S(1)}, f32[64,256]{1,0:T(8,128)S(1)}, u32[]{:S(2)}, u32[]{:S(2)}) collective-permute-start(f32[64,256]{1,0:T(8,128)S(1)} %get-tuple-element.6), channel_id=1, source_target_pairs={{0,128},{128,256},{256,384},{1,129},{129,257},{257,385},{2,130},{1... | collective-permute-start | bytes 196616 | tf_op jit(solution)/shard_map/ppermute | solution.py:124
  4.9 0.7 fusion.1
  5.6 0.1 dynamic_update_slice.3.label_ref
  5.7 0.0 collective-permute-done.1.after_ref
  5.8 4.0 %collective-permute-done.before_ref = f32[64,256]{1,0:T(8,128)S(1)} collective-permute-done((f32[64,256]{1,0:T(8,128)S(1)}, f32[64,256]{1,0:T(8,128)S(1)}, u32[]{:S(2)}, u32[]{:S(2)}) %collective-permute-start) | collective-permute-done | bytes 65568 | tf_op jit(solution)/shard_map/ppermute | solution.py:124
  9.8 0.0 copy-start
  9.8 0.9 %copy-done = f32[64,1024]{1,0:T(8,128)S(1)} copy-done((f32[64,1024]{1,0:T(8,128)S(1)}, f32[64,1024]{1,0:T(8,128)}, u32[]{:S(2)}) %copy-start) | copy-done | bytes 262168
  10.7 0.0 copy-start.1
  10.7 0.9 %copy-done.1 = s32[64,1024]{1,0:T(8,128)S(1)} copy-done((s32[64,1024]{1,0:T(8,128)S(1)}, s32[64,1024]{1,0:T(8,128)}, u32[]{:S(2)}) %copy-start.1) | copy-done | bytes 262168
  11.7 0.0 copy-start.2
  11.7 0.7 copy-done.2
  12.4 2.7 %correct.1 = f32[4,520,128]{2,1,0:T(8,128)} custom-call(s32[1]{0:T(128)} %bitcast.1.last_ref, f32[64,1024]{1,0:T(8,128)S(1)} %copy-done, f32[64,256]{1,0:T(8,128)S(1)} %collective-permute-done.before_ref, f32[64,256]{1,0:T(8,128)S(1)} %collective-permute-done.1.after_ref, f32[1,256]{1,0:T(1,128)S(1)} %copy-done.2, ...), custom_call_target="tpu_custom_call" | custom-call | tf_op jit(solution)/shard_map/correct/pallas_call | solution.py:111
  15.1 4.5 %all-to-all-start = ((f32[4,520,128]{2,1,0:T(8,128)}), f32[4,520,128]{2,1,0:T(8,128)S(1)}, u32[]{:S(2)}, u32[]{:S(2)}) async-start(f32[4,520,128]{2,1,0:T(8,128)} %correct.1), calls=%async_computation | async-start | bytes 2129920 | tf_op jit(solution)/shard_map/all_to_all | solution.py:141
  19.5 13.8 %all-to-all-done.arrived_ref = f32[4,520,128]{2,1,0:T(8,128)S(1)} async-done(((f32[4,520,128]{2,1,0:T(8,128)}), f32[4,520,128]{2,1,0:T(8,128)S(1)}, u32[]{:S(2)}, u32[]{:S(2)}) %all-to-all-start) | async-done | bytes 1064992 | tf_op jit(solution)/shard_map/all_to_all | solution.py:141
  33.4 0.5 combine_other.1
  33.8 1.9 %collective-permute-start.2 = (f32[16,72,128]{2,1,0:T(8,128)S(1)}, f32[16,72,128]{2,1,0:T(8,128)S(1)}, u32[]{:S(2)}, u32[]{:S(2)}) collective-permute-start(f32[16,72,128]{2,1,0:T(8,128)S(1)} %combine_other.1), channel_id=1, source_target_pairs={{0,1},{1,0},{2,3},{3,2},{4,5},{5,4},{6,7},{7,6},{8,9},{9,8},{10,11... | collective-permute-start | bytes 1769480 | tf_op jit(solution)/shard_map/ppermute | solution.py:148
  35.8 2.0 %collective-permute-done.2.refs_0_ = f32[16,72,128]{2,1,0:T(8,128)S(1)} collective-permute-done((f32[16,72,128]{2,1,0:T(8,128)S(1)}, f32[16,72,128]{2,1,0:T(8,128)S(1)}, u32[]{:S(2)}, u32[]{:S(2)}) %collective-permute-start.2) | collective-permute-done | bytes 589856 | tf_op jit(solution)/shard_map/ppermute | solution.py:148
  37.7 0.5 combine_own.1
  38.2 50.1 %all_to_all.10.arrived_ref = f32[16,72,128]{2,1,0:T(8,128)S(1)} all-to-all(f32[16,72,128]{2,1,0:T(8,128)S(1)} %combine_own.1), channel_id=1, replica_groups=mesh['section'=4,'y'=4,'z'=16,'c'=2] {'z'}, dimensions={0} | all-to-all | bytes 1179648 | tf_op jit(solution)/shard_map/all_to_all | solution.py:150
  88.3 0.7 finish.1
  (1 shorter events, 0.0 us)
Async XLA Ops:
  0.9 4.9 %collective-permute-start.1 = (f32[64,256]{1,0:T(8,128)S(1)}, f32[64,256]{1,0:T(8,128)S(1)}, u32[]{:S(2)}, u32[]{:S(2)}) collective-permute-start(f32[64,256]{1,0:T(8,128)S(1)} %get-tuple-element.5), channel_id=1, source_target_pairs={{128,0},{256,128},{384,256},{129,1},{257,129},{385,257},{130,2},{2... | collective-permute-start | bytes 196616 | tf_op jit(solution)/shard_map/ppermute | solution.py:124
  3.6 6.2 %collective-permute-start = (f32[64,256]{1,0:T(8,128)S(1)}, f32[64,256]{1,0:T(8,128)S(1)}, u32[]{:S(2)}, u32[]{:S(2)}) collective-permute-start(f32[64,256]{1,0:T(8,128)S(1)} %get-tuple-element.6), channel_id=1, source_target_pairs={{0,128},{128,256},{256,384},{1,129},{129,257},{257,385},{2,130},{1... | collective-permute-start | bytes 196616 | tf_op jit(solution)/shard_map/ppermute | solution.py:124
  9.8 1.0 %copy-start = (f32[64,1024]{1,0:T(8,128)S(1)}, f32[64,1024]{1,0:T(8,128)}, u32[]{:S(2)}) copy-start(f32[64,1024]{1,0:T(8,128)} %traces_ref.1) | copy-start | bytes 786436
  10.7 0.9 %copy-start.1 = (s32[64,1024]{1,0:T(8,128)S(1)}, s32[64,1024]{1,0:T(8,128)}, u32[]{:S(2)}) copy-start(s32[64,1024]{1,0:T(8,128)} %map_ref.1) | copy-start | bytes 786436
  11.7 0.7 copy-start.2
  15.1 18.3 %all-to-all-start = ((f32[4,520,128]{2,1,0:T(8,128)}), f32[4,520,128]{2,1,0:T(8,128)S(1)}, u32[]{:S(2)}, u32[]{:S(2)}) async-start(f32[4,520,128]{2,1,0:T(8,128)} %correct.1), calls=%async_computation | async-start | bytes 2129920 | tf_op jit(solution)/shard_map/all_to_all | solution.py:141
  33.8 3.9 %collective-permute-start.2 = (f32[16,72,128]{2,1,0:T(8,128)S(1)}, f32[16,72,128]{2,1,0:T(8,128)S(1)}, u32[]{:S(2)}, u32[]{:S(2)}) collective-permute-start(f32[16,72,128]{2,1,0:T(8,128)S(1)} %combine_other.1), channel_id=1, source_target_pairs={{0,1},{1,0},{2,3},{3,2},{4,5},{5,4},{6,7},{7,6},{8,9},{9,8},{10,11... | collective-permute-start | bytes 1769480 | tf_op jit(solution)/shard_map/ppermute | solution.py:148

commit v2 on v1

v2 whole, which is shorter than its diff:
```python
import functools

import jax
import jax.numpy as jnp
from jax import lax
from jax.experimental import pallas as pl
from jax.experimental.pallas import tpu as pltpu
from jax.sharding import Mesh
from jax.sharding import PartitionSpec as P

BIN_DEV = 8
CAP = 2
LANES = 128
NY, NU, NW, NC = 4, 8, 2, 2
BINS = ("y", "u", "w", "c")
NEAR = ("y", "w", "c")
PEERS = NY * NW * NC
SLOTS = NU * CAP


def halves(value):
    high = value.astype(jnp.bfloat16)
    low = (value - high.astype(jnp.float32)).astype(jnp.bfloat16)
    return high, low


def dot(a, b):
    return jnp.dot(a, b, preferred_element_type=jnp.float32)


def dot_split(a, b):
    return dot(a[0], b[0]) + (dot(a[1], b[0]) + dot(a[0], b[1]))


def move_out(window, quarters):
    rows, span = window.shape
    step = pltpu.roll(window, span - 1, 1) - window
    lane = lax.broadcasted_iota(jnp.int32, (rows, LANES), 1)
    moved = []
    for c, quarter in enumerate(quarters):
        place = lane + (quarter >> 2)
        weight = (quarter & 3).astype(jnp.float32) * 0.25
        inside = place & (LANES - 1)
        block = place >> 7
        near = slope = None
        for k in range(3):
            columns = slice((c + k) * LANES, (c + k + 1) * LANES)
            value = jnp.take_along_axis(window[:, columns], inside, axis=1, mode="promise_in_bounds")
            change = jnp.take_along_axis(step[:, columns], inside, axis=1, mode="promise_in_bounds")
            near = value if k == 0 else jnp.where(block == k, value, near)
            slope = change if k == 0 else jnp.where(block == k, change, slope)
        moved.append(near + weight * slope)
    return jnp.concatenate(moved, axis=1)


def place_slots(slot, moved, target_ref, start):
    rows = moved.shape[0]
    number = lax.broadcasted_iota(jnp.int32, (PEERS * SLOTS, rows), 0)
    member = jnp.where(number == slot, 1.0, 0.0).astype(jnp.bfloat16)
    high, low = halves(moved)
    placed = dot(member, high) + dot(member, low)
    for c in range(moved.shape[1] // LANES):
        piece = placed[:, c * LANES : (c + 1) * LANES].reshape(PEERS, SLOTS, LANES)
        target_ref[:, start + c * SLOTS : start + (c + 1) * SLOTS, :] = piece


def inner_kernel(
    place_ref, traces_hbm, map_hbm, filter_hbm, owner_hbm, sub_hbm,
    out_hbm, high_ref, low_ref, edge_ref, edge_map_ref, slot_ref,
    traces_ref, map_ref, filter_ref, owner_ref, sub_ref, stage_ref, sems, out_sems,
):
    rows, width = traces_ref.shape
    taps = filter_ref.shape[1]
    half = width // 2
    loads = [
        pltpu.make_async_copy(filter_hbm, filter_ref, sems.at[0]),
        pltpu.make_async_copy(owner_hbm, owner_ref, sems.at[1]),
        pltpu.make_async_copy(sub_hbm, sub_ref, sems.at[2]),
        pltpu.make_async_copy(traces_hbm, traces_ref, sems.at[3]),
        pltpu.make_async_copy(map_hbm.at[:, taps : taps + half], map_ref, sems.at[4]),
        pltpu.make_async_copy(map_hbm.at[:, :taps], edge_map_ref.at[:, :taps], sems.at[5]),
        pltpu.make_async_copy(map_hbm.at[:, taps + half :], edge_map_ref.at[:, taps:], sems.at[6]),
    ]
    for load in loads:
        load.start()
    loads[0].wait()
    padded = jnp.concatenate([filter_ref[...], jnp.zeros((1, taps), jnp.float32)], axis=1)
    shifted = pltpu.roll(jnp.broadcast_to(padded, (taps, 2 * taps)), 0, 1, stride=1, stride_axis=0)
    toeplitz = halves(shifted)
    high_ref[...], low_ref[...] = toeplitz

    loads[1].wait()
    loads[2].wait()
    owner, sub = owner_ref[...], sub_ref[...]
    owners = NY * NU * NW * NC
    named = lax.broadcasted_iota(jnp.int32, (owners, rows), 0) == owner
    named = jnp.where(named, 1.0, 0.0)
    earlier = lax.broadcasted_iota(jnp.int32, (rows, rows), 0) < lax.broadcasted_iota(jnp.int32, (rows, rows), 1)
    earlier = jnp.where(earlier, 1.0, 0.0).astype(jnp.bfloat16)
    rank = jnp.sum(named * dot(named.astype(jnp.bfloat16), earlier), axis=0, keepdims=True).astype(jnp.int32)
    core, w = owner % NC, owner // NC % NW
    u, y = owner // (NC * NW) % NU, owner // (NC * NW * NU)
    peer = (y * NW + w) * NC + core
    within = u * CAP + rank
    slot = peer * SLOTS + within
    slot_ref[...] = slot
    to_peer = lax.broadcasted_iota(jnp.int32, (PEERS, rows), 0) == peer
    to_peer = jnp.where(to_peer, (sub + 1).astype(jnp.float32), 0.0).astype(jnp.bfloat16)
    column = lax.broadcasted_iota(jnp.int32, (PEERS * SLOTS, rows), 0)
    in_column = jnp.where(column == within + place_ref[0] * SLOTS, 1.0, 0.0).astype(jnp.bfloat16)
    labels = lax.dot_general(to_peer, in_column, (((1,), (1,)), ((), ())), preferred_element_type=jnp.float32)
    first = lax.broadcasted_iota(jnp.int32, (PEERS, BIN_DEV, LANES), 1) == 0
    stage_ref[:, half // LANES * SLOTS :, :] = jnp.where(
        first, labels[:, None, :LANES], labels[:, None, LANES:]
    )

    loads[3].wait()
    count = width // taps
    stacked = jnp.concatenate([traces_ref[:, b * taps : (b + 1) * taps] for b in range(count)], axis=0)
    spread = dot_split(halves(stacked), toeplitz)
    pieces = [
        spread[b * rows : (b + 1) * rows, :taps] + spread[(b - 1) * rows : b * rows, taps:] for b in range(1, count)
    ]
    edge_ref[:, :taps] = spread[:rows, :taps]
    edge_ref[:, taps : 2 * taps] = pieces[0]
    edge_ref[:, 2 * taps : 3 * taps] = pieces[-1]
    edge_ref[:, 3 * taps :] = spread[(count - 1) * rows :, taps:]
    loads[4].wait()
    quarters = [map_ref[:, c * LANES : (c + 1) * LANES] for c in range(half // LANES)]
    place_slots(slot, move_out(jnp.concatenate(pieces, axis=1), quarters), stage_ref, 0)
    body = half // LANES * SLOTS
    start = taps // LANES * SLOTS
    stores = [
        pltpu.make_async_copy(stage_ref.at[:, :body, :], out_hbm.at[:, start : start + body, :], out_sems.at[0]),
        pltpu.make_async_copy(stage_ref.at[:, body:, :], out_hbm.at[:, 2 * body :, :], out_sems.at[1]),
    ]
    for store in stores:
        store.start()
    loads[5].wait()
    loads[6].wait()
    for store in stores:
        store.wait()


def outer_kernel(
    last_ref, before_ref, after_ref, high_ref, low_ref, edge_ref, edge_map_ref, slot_ref, given_hbm,
    out_hbm, stage_ref, out_sems,
):
    rows, taps = before_ref.shape
    body = taps // LANES * SLOTS
    slot = slot_ref[...]
    early = dot_split(halves(before_ref[...]), (high_ref[:, taps:], low_ref[:, taps:])) + edge_ref[:, :taps]
    window = jnp.concatenate([early, edge_ref[:, taps : 2 * taps]], axis=1)
    quarters = [edge_map_ref[:, c * LANES : (c + 1) * LANES] for c in range(taps // LANES)]
    place_slots(slot, move_out(window, quarters), stage_ref, 0)
    first = pltpu.make_async_copy(stage_ref.at[:, :body, :], out_hbm.at[:, :body, :], out_sems.at[0])
    first.start()
    late = dot_split(halves(after_ref[...]), (high_ref[:, :taps], low_ref[:, :taps])) + edge_ref[:, 3 * taps :]
    late = jnp.where(last_ref[0] == 1, 0.0, late)
    window = jnp.concatenate([edge_ref[:, 2 * taps : 3 * taps], late], axis=1)
    quarters = [edge_map_ref[:, taps + c * LANES : taps + (c + 1) * LANES] for c in range(taps // LANES)]
    place_slots(slot, move_out(window, quarters), stage_ref, body)
    second = pltpu.make_async_copy(stage_ref.at[:, body:, :], out_hbm.at[:, 3 * body : 4 * body, :], out_sems.at[1])
    second.start()
    first.wait()
    second.wait()


def combine_kernel(arrived_ref, out_ref):
    parts = out_ref.shape[1] // BIN_DEV - 1
    tile = arrived_ref[0, parts * SLOTS :, :]
    for peer in range(1, PEERS):
        tile = tile + arrived_ref[peer, parts * SLOTS :, :]
    labels = jnp.concatenate([tile[0:1, :], tile[1:2, :]], axis=1)
    shape = (NU * BIN_DEV, PEERS * SLOTS)
    row = lax.broadcasted_iota(jnp.int32, shape, 0)
    column = lax.broadcasted_iota(jnp.int32, shape, 1)
    bin_label = (row % BIN_DEV + 1).astype(jnp.float32)
    hit = (labels == bin_label) & (row // BIN_DEV == column % SLOTS // CAP)
    member = jnp.where(hit, 1.0, 0.0).astype(jnp.bfloat16)
    for c in range(0, parts, 2):
        piece = jnp.concatenate(
            [
                arrived_ref[:, k * SLOTS : (k + 1) * SLOTS, :].reshape(PEERS * SLOTS, LANES)
                for k in (c, c + 1)
            ],
            axis=1,
        )
        high, low = halves(piece)
        total = dot(member, high) + dot(member, low)
        for k in (0, 1):
            out_ref[:, (c + k) * BIN_DEV : (c + k + 1) * BIN_DEV, :] = total[
                :, k * LANES : (k + 1) * LANES
            ].reshape(NU, BIN_DEV, LANES)
    fold = dot(member, jnp.ones((PEERS * SLOTS, LANES), jnp.bfloat16))
    out_ref[:, parts * BIN_DEV :, :] = fold.reshape(NU, BIN_DEV, LANES)


def finish_kernel(arrived_ref, out_ref):
    total = arrived_ref[0]
    for u in range(1, NU):
        total = total + arrived_ref[u]
    parts = total.shape[0] // BIN_DEV - 1
    scale = jnp.sqrt(jnp.maximum(total[parts * BIN_DEV :, :], 1.0))
    for c in range(parts):
        out_ref[:, c * LANES : (c + 1) * LANES] = total[c * BIN_DEV : (c + 1) * BIN_DEV, :] / scale


VMEM = pl.BlockSpec(memory_space=pltpu.VMEM)
SMEM = pl.BlockSpec(memory_space=pltpu.SMEM)
ANY = pl.BlockSpec(memory_space=pl.ANY)
LIMIT = 24 * 1024 * 1024


def f32(*shape):
    return jax.ShapeDtypeStruct(shape, jnp.float32)


def correct_inner(place, traces, sample_map, filters, owner, sub):
    rows, width = traces.shape
    taps = filters.shape[1]
    length = (width // LANES) * SLOTS + BIN_DEV
    return pl.pallas_call(
        inner_kernel,
        out_shape=(
            f32(PEERS, length, LANES),
            jax.ShapeDtypeStruct((taps, 2 * taps), jnp.bfloat16),
            jax.ShapeDtypeStruct((taps, 2 * taps), jnp.bfloat16),
            f32(rows, 4 * taps),
            jax.ShapeDtypeStruct((rows, 2 * taps), jnp.int32),
            jax.ShapeDtypeStruct((1, rows), jnp.int32),
        ),
        in_specs=[SMEM] + [ANY] * 5,
        out_specs=(ANY, VMEM, VMEM, VMEM, VMEM, VMEM),
        scratch_shapes=[
            pltpu.VMEM((rows, width), jnp.float32),
            pltpu.VMEM((rows, width // 2), jnp.int32),
            pltpu.VMEM((1, taps), jnp.float32),
            pltpu.VMEM((1, rows), jnp.int32),
            pltpu.VMEM((1, rows), jnp.int32),
            pltpu.VMEM((PEERS, width // 2 // LANES * SLOTS + BIN_DEV, LANES), jnp.float32),
            pltpu.SemaphoreType.DMA((7,)),
            pltpu.SemaphoreType.DMA((2,)),
        ],
        name="correct_inner",
        cost_estimate=pl.CostEstimate(flops=500_000_000, bytes_accessed=2_000_000, transcendentals=0),
        compiler_params=pltpu.CompilerParams(vmem_limit_bytes=LIMIT),
    )(place, traces, sample_map, filters, owner, sub)


def correct_outer(last, before, after, high, low, edge, edge_map, slot, given):
    taps = before.shape[1]
    return pl.pallas_call(
        outer_kernel,
        out_shape=jax.ShapeDtypeStruct(given.shape, given.dtype),
        in_specs=[SMEM] + [VMEM] * 7 + [ANY],
        out_specs=ANY,
        input_output_aliases={8: 0},
        scratch_shapes=[
            pltpu.VMEM((PEERS, 2 * taps // LANES * SLOTS, LANES), jnp.float32),
            pltpu.SemaphoreType.DMA((2,)),
        ],
        name="correct_outer",
        compiler_params=pltpu.CompilerParams(vmem_limit_bytes=LIMIT),
    )(last, before, after, high, low, edge, edge_map, slot, given)


def on_vmem(kernel, shape, name, operand):
    return pl.pallas_call(
        kernel,
        out_shape=f32(*shape),
        in_specs=[VMEM],
        out_specs=VMEM,
        name=name,
        compiler_params=pltpu.CompilerParams(vmem_limit_bytes=LIMIT),
    )(operand)


def passed_along(value, axis, steps):
    count = lax.axis_size(axis)
    leading, last = (max(0, -steps), min(count, count - steps))
    return lax.ppermute(value, axis, [(source, source + steps) for source in range(leading, last)])


def per_device(traces, filters, owners, sub_bins, sample_map):
    rows, width = traces.shape
    taps = filters.shape[1]
    before = passed_along(traces[:, width - taps :], "section", 1)
    after = passed_along(traces[:, :taps], "section", -1)
    place = lax.axis_index(NEAR).astype(jnp.int32).reshape(1)
    last = (lax.axis_index("section") == lax.axis_size("section") - 1).astype(jnp.int32).reshape(1)
    sent, *kept = correct_inner(
        place, traces, sample_map, filters, owners.reshape(1, rows), sub_bins.reshape(1, rows)
    )
    sent = correct_outer(last, before, after, *kept, sent)
    near = lax.all_to_all(sent, NEAR, split_axis=0, concat_axis=0, tiled=True)
    summed = on_vmem(combine_kernel, (NU, (width // LANES + 1) * BIN_DEV, LANES), "combine", near)
    arrived = lax.all_to_all(summed, "u", split_axis=0, concat_axis=0, tiled=True)
    return on_vmem(finish_kernel, (BIN_DEV, width), "finish", arrived)


def solution(mesh):
    fine = Mesh(mesh.devices.reshape(mesh.devices.shape[0], NY, NU, NW, NC), ("section",) + BINS)
    in_specs = (
        P(BINS, "section"),
        P(BINS, None),
        P(BINS, None),
        P(BINS),
        P(BINS, "section"),
    )
    return jax.shard_map(
        per_device, mesh=fine, in_specs=in_specs, out_specs=P(BINS, "section"), check_vma=False
    )
```

time: 89.4 us -> 75.7 us (0.85)
  the two profiles are of different devices: /device:TPU:6 before, /device:TPU:2 now
where the time goes in v2:
time: 75.7 us; the launch traced here: 75.4 us
  blocking collectives  56.2 us (74%)
  starting transfers between devices  9.74 us (13%)
  local copies, waits for them, and re-layouts  4.76 us (6%)
  Pallas kernels  4.62 us (6%)
    all_to_all x1, blocking collectives, per_device(): lax.all_to_all(summed, 'u', split_axis=0, concat_axis=0, tiled=True)  36.4 us
    all_to_all x1, blocking collectives, per_device(): near = lax.all_to_all(sent, NEAR, split_axis=0, concat_axis=0, tiled=True)  19.8 us
    ppermute x2, starting transfers between devices, passed_along(): lax.ppermute(value, axis, [(source, source + steps) for source in range(l...  9.74 us
    unnamed x10, local copies, waits for them, and re-layouts  3.88 us
    pallas_call x1, Pallas kernels, correct_inner(): pl.pallas_call(inner_kernel, out_shape=(f32(PEERS, length, LANES), jax.Sh...  2.15 us
  transfers between devices with their start and end apart: 2, of which 0 were waited for; matrix products, arithmetic and copies ran while one was open for 0% of the time, Pallas kernels for 3%

profile of v2, /device:TPU:2, one launch (start us, length us, event | category | flops | bytes accessed | tf_op | source)
XLA Modules:
  0.0 75.4 jit_solution(15231480518543417097)
XLA Ops:
  0.0 0.9 %fusion = (f32[64,256]{1,0:T(8,128)S(1)}, f32[64,256]{1,0:T(8,128)S(1)}) fusion(f32[64,1024]{1,0:T(8,128)} %traces_hbm.1), kind=kLoop, calls=%fused_computation | loop fusion | bytes 262144 | tf_op jit(solution)/shard_map/slice | solution.py:289
  0.9 7.8 %collective-permute-start.1 = (f32[64,256]{1,0:T(8,128)S(1)}, f32[64,256]{1,0:T(8,128)S(1)}, u32[]{:S(2)}, u32[]{:S(2)}) collective-permute-start(f32[64,256]{1,0:T(8,128)S(1)} %get-tuple-element.17), channel_id=1, source_target_pairs={{128,0},{256,128},{384,256},{129,1},{257,129},{385,257},{130,2},{2... | collective-permute-start | bytes 196616 | tf_op jit(solution)/shard_map/ppermute | solution.py:282
  8.7 1.9 %collective-permute-start = (f32[64,256]{1,0:T(8,128)S(1)}, f32[64,256]{1,0:T(8,128)S(1)}, u32[]{:S(2)}, u32[]{:S(2)}) collective-permute-start(f32[64,256]{1,0:T(8,128)S(1)} %get-tuple-element.18), channel_id=1, source_target_pairs={{0,128},{128,256},{256,384},{1,129},{129,257},{257,385},{2,130},{1... | collective-permute-start | bytes 196616 | tf_op jit(solution)/shard_map/ppermute | solution.py:282
  10.6 0.0 copy-start
  10.7 0.9 %copy-done = f32[64,1024]{1,0:T(8,128)S(1)} copy-done((f32[64,1024]{1,0:T(8,128)S(1)}, f32[64,1024]{1,0:T(8,128)}, u32[]{:S(2)}) %copy-start) | copy-done | bytes 262168
  11.6 0.0 copy-start.1
  11.6 0.9 %copy-done.1 = s32[64,1024]{1,0:T(8,128)S(1)} copy-done((s32[64,1024]{1,0:T(8,128)S(1)}, s32[64,1024]{1,0:T(8,128)}, u32[]{:S(2)}) %copy-start.1) | copy-done | bytes 262168
  12.6 0.0 copy-start.2
  12.6 0.7 copy-done.2
  13.2 0.0 copy-start.3
  13.2 0.7 copy-done.3
  13.9 0.0 copy-start.4
  13.9 0.7 copy-done.4
  14.5 2.2 %correct_inner.1 = (f32[16,136,128]{2,1,0:T(8,128)S(1)}, bf16[256,512]{1,0:T(8,128)(2,1)S(1)}, bf16[256,512]{1,0:T(8,128)(2,1)S(1)}, f32[64,1024]{1,0:T(8,128)S(...) custom-call(s32[1]{0:T(128)} %bitcast.1.place_ref, f32[64,1024]{1,0:T(8,128)S(1)} %copy-done, s32[64,1024]{1,0:T(8,128)S(1)} %copy-done.1, ...), custom_call_target="tpu_custom_call" | custom-call | flops 500000000 | bytes 2000000 | tf_op jit(solution)/shard_map/correct_inner/pallas_call | solution.py:223
  16.7 0.0 collective-permute-done.1.after_ref
  16.7 0.0 collective-permute-done.before_ref
  16.7 1.5 %correct_outer.1 = f32[16,136,128]{2,1,0:T(8,128)S(1)} custom-call(s32[1]{0:T(128)} %bitcast.last_ref, f32[64,256]{1,0:T(8,128)S(1)} %collective-permute-done.before_ref, f32[64,256]{1,0:T(8,128)S(1)} %collective-permute-done.1.after_ref, bf16[256,512]{1,0:T(8,128)(2,1)S(1)} %get-tuple-element.11.high_ref, ...), custom_call_target="tpu_custom_call", output_to_operand_aliasing={{}: (8, {})} | custom-call | tf_op jit(solution)/shard_map/correct_outer/pallas_call | solution.py:253
  18.2 19.8 %all_to_all.10.arrived_ref = f32[16,136,128]{2,1,0:T(8,128)S(1)} all-to-all(f32[16,136,128]{2,1,0:T(8,128)S(1)} %correct_outer.1), channel_id=1, replica_groups=mesh['section'=4,'y'=4,'u'=8,'w'=2,'c'=2] {'y','w','c'}, dimensions={0} | all-to-all | bytes 2228224 | tf_op jit(solution)/shard_map/all_to_all | solution.py:296
  38.0 0.4 combine.1
  38.3 36.4 %all_to_all.11.arrived_ref = f32[8,72,128]{2,1,0:T(8,128)S(1)} all-to-all(f32[8,72,128]{2,1,0:T(8,128)S(1)} %combine.1), channel_id=1, replica_groups=mesh['section'=4,'y'=4,'u'=8,'w'=2,'c'=2] {'u'}, dimensions={0} | all-to-all | bytes 589824 | tf_op jit(solution)/shard_map/all_to_all | solution.py:298
  74.7 0.6 finish.1
Async XLA Ops:
  0.9 15.8 %collective-permute-start.1 = (f32[64,256]{1,0:T(8,128)S(1)}, f32[64,256]{1,0:T(8,128)S(1)}, u32[]{:S(2)}, u32[]{:S(2)}) collective-permute-start(f32[64,256]{1,0:T(8,128)S(1)} %get-tuple-element.17), channel_id=1, source_target_pairs={{128,0},{256,128},{384,256},{129,1},{257,129},{385,257},{130,2},{2... | collective-permute-start | bytes 196616 | tf_op jit(solution)/shard_map/ppermute | solution.py:282
  8.7 8.0 %collective-permute-start = (f32[64,256]{1,0:T(8,128)S(1)}, f32[64,256]{1,0:T(8,128)S(1)}, u32[]{:S(2)}, u32[]{:S(2)}) collective-permute-start(f32[64,256]{1,0:T(8,128)S(1)} %get-tuple-element.18), channel_id=1, source_target_pairs={{0,128},{128,256},{256,384},{1,129},{129,257},{257,385},{2,130},{1... | collective-permute-start | bytes 196616 | tf_op jit(solution)/shard_map/ppermute | solution.py:282
  10.6 1.0 %copy-start = (f32[64,1024]{1,0:T(8,128)S(1)}, f32[64,1024]{1,0:T(8,128)}, u32[]{:S(2)}) copy-start(f32[64,1024]{1,0:T(8,128)} %traces_hbm.1) | copy-start | bytes 786436
  11.6 0.9 %copy-start.1 = (s32[64,1024]{1,0:T(8,128)S(1)}, s32[64,1024]{1,0:T(8,128)}, u32[]{:S(2)}) copy-start(s32[64,1024]{1,0:T(8,128)} %map_hbm.1) | copy-start | bytes 786436
  12.6 0.7 copy-start.2
  13.2 0.7 copy-start.3
  13.9 0.7 copy-start.4

commit v3 on v2

v3 whole, which is shorter than its diff:
```python
import jax
import jax.numpy as jnp
from jax import lax
from jax.experimental import pallas as pl
from jax.experimental.pallas import tpu as pltpu
from jax.sharding import Mesh
from jax.sharding import PartitionSpec as P

BIN_DEV = 8
CAP = 2
LANES = 128
NY, NU, NW, NC = 4, 8, 2, 2
BINS = ("y", "u", "w", "c")
NEAR = ("y", "w", "c")
PEERS = NY * NW * NC
SLOTS = NU * CAP


def halves(value):
    high = value.astype(jnp.bfloat16)
    low = (value - high.astype(jnp.float32)).astype(jnp.bfloat16)
    return high, low


def dot(a, b):
    return jnp.dot(a, b, preferred_element_type=jnp.float32)


def dot_split(a, b):
    return dot(a[0], b[0]) + (dot(a[1], b[0]) + dot(a[0], b[1]))


def move_out(window, quarters):
    rows, span = window.shape
    step = pltpu.roll(window, span - 1, 1) - window
    lane = lax.broadcasted_iota(jnp.int32, (rows, LANES), 1)
    moved = []
    for c, quarter in enumerate(quarters):
        place = lane + (quarter >> 2)
        weight = (quarter & 3).astype(jnp.float32) * 0.25
        inside = place & (LANES - 1)
        block = place >> 7
        near = slope = None
        for k in range(3):
            columns = slice((c + k) * LANES, (c + k + 1) * LANES)
            value = jnp.take_along_axis(window[:, columns], inside, axis=1, mode="promise_in_bounds")
            change = jnp.take_along_axis(step[:, columns], inside, axis=1, mode="promise_in_bounds")
            near = value if k == 0 else jnp.where(block == k, value, near)
            slope = change if k == 0 else jnp.where(block == k, change, slope)
        moved.append(near + weight * slope)
    return jnp.concatenate(moved, axis=1)


def correct_kernel(
    filter_ref, code_ref, traces_hbm, map_hbm, before_ref, after_ref,
    out_hbm, traces_ref, map_ref, stage_ref, sems, out_sems,
):
    rows, width = traces_ref.shape
    taps = before_ref.shape[1]
    count = width // taps
    loads = []
    for k, (source, target) in enumerate([(traces_hbm, traces_ref), (map_hbm, map_ref)]):
        for half in range(2):
            columns = pl.ds(half * (width // 2), width // 2)
            loads.append(
                pltpu.make_async_copy(source.at[:, columns], target.at[:, columns], sems.at[2 * k + half])
            )
    for load in loads:
        load.start()
    shifted = pltpu.roll(jnp.broadcast_to(filter_ref[...], (taps, 2 * taps)), 0, 1, stride=1, stride_axis=0)
    toeplitz = halves(shifted)

    owner = code_ref[...] // BIN_DEV
    sub = code_ref[...] % BIN_DEV
    owners = NY * NU * NW * NC
    named = lax.broadcasted_iota(jnp.int32, (owners, rows), 0) == owner
    named = jnp.where(named, 1.0, 0.0)
    earlier = lax.broadcasted_iota(jnp.int32, (rows, rows), 0) < lax.broadcasted_iota(jnp.int32, (rows, rows), 1)
    earlier = jnp.where(earlier, 1.0, 0.0).astype(jnp.bfloat16)
    rank = jnp.sum(named * dot(named.astype(jnp.bfloat16), earlier), axis=0, keepdims=True).astype(jnp.int32)
    core, w = owner % NC, owner // NC % NW
    u, y = owner // (NC * NW) % NU, owner // (NC * NW * NU)
    peer = (y * NW + w) * NC + core
    within = u * CAP + rank
    number = lax.broadcasted_iota(jnp.int32, (PEERS * SLOTS, rows), 0)
    member = jnp.where(number == peer * SLOTS + within, 1.0, 0.0).astype(jnp.bfloat16)
    to_peer = lax.broadcasted_iota(jnp.int32, (PEERS, rows), 0) == peer
    to_peer = jnp.where(to_peer, (sub + 1).astype(jnp.float32), 0.0).astype(jnp.bfloat16)
    in_column = jnp.where(number == within + lax.axis_index(NEAR) * SLOTS, 1.0, 0.0).astype(jnp.bfloat16)
    labels = lax.dot_general(to_peer, in_column, (((1,), (1,)), ((), ())), preferred_element_type=jnp.float32)
    first = lax.broadcasted_iota(jnp.int32, (PEERS, BIN_DEV, LANES), 1) == 0
    body = taps // LANES * SLOTS
    stage_ref[:, count * body :, :] = jnp.where(first, labels[:, None, :LANES], labels[:, None, LANES:])

    def store(k, extent):
        part = pl.ds(k * body, extent)
        return pltpu.make_async_copy(stage_ref.at[:, part, :], out_hbm.at[:, part, :], out_sems.at[k])

    stores = [store(count, BIN_DEV)]
    stores[0].start()

    loads[0].wait()
    loads[1].wait()
    stacked = [before_ref[...]] + [traces_ref[:, b * taps : (b + 1) * taps] for b in range(count)] + [after_ref[...]]
    spread = dot_split(halves(jnp.concatenate(stacked, axis=0)), toeplitz)
    pieces = [
        spread[b * rows : (b + 1) * rows, :taps] + spread[(b - 1) * rows : b * rows, taps:]
        for b in range(1, count + 2)
    ]
    pieces[-1] = jnp.where(lax.axis_index("section") == lax.axis_size("section") - 1, 0.0, pieces[-1])
    loads[2].wait()
    loads[3].wait()
    for k in range(count):
        quarters = [map_ref[:, k * taps + c * LANES : k * taps + (c + 1) * LANES] for c in range(taps // LANES)]
        moved = move_out(jnp.concatenate(pieces[k : k + 2], axis=1), quarters)
        high, low = halves(moved)
        placed = dot(member, high) + dot(member, low)
        for c in range(taps // LANES):
            stage_ref[:, k * body + c * SLOTS : k * body + (c + 1) * SLOTS, :] = placed[
                :, c * LANES : (c + 1) * LANES
            ].reshape(PEERS, SLOTS, LANES)
        stores.append(store(k, body))
        stores[-1].start()
    for one in stores:
        one.wait()


def combine_kernel(arrived_ref, out_ref):
    parts = out_ref.shape[1] // BIN_DEV - 1
    tile = arrived_ref[0, parts * SLOTS :, :]
    for peer in range(1, PEERS):
        tile = tile + arrived_ref[peer, parts * SLOTS :, :]
    labels = jnp.concatenate([tile[0:1, :], tile[1:2, :]], axis=1)
    shape = (NU * BIN_DEV, PEERS * SLOTS)
    row = lax.broadcasted_iota(jnp.int32, shape, 0)
    column = lax.broadcasted_iota(jnp.int32, shape, 1)
    bin_label = (row % BIN_DEV + 1).astype(jnp.float32)
    hit = (labels == bin_label) & (row // BIN_DEV == column % SLOTS // CAP)
    member = jnp.where(hit, 1.0, 0.0).astype(jnp.bfloat16)
    for c in range(0, parts, 2):
        piece = jnp.concatenate(
            [
                arrived_ref[:, k * SLOTS : (k + 1) * SLOTS, :].reshape(PEERS * SLOTS, LANES)
                for k in (c, c + 1)
            ],
            axis=1,
        )
        high, low = halves(piece)
        total = dot(member, high) + dot(member, low)
        for k in (0, 1):
            out_ref[:, (c + k) * BIN_DEV : (c + k + 1) * BIN_DEV, :] = total[
                :, k * LANES : (k + 1) * LANES
            ].reshape(NU, BIN_DEV, LANES)
    fold = dot(member, jnp.ones((PEERS * SLOTS, LANES), jnp.bfloat16))
    out_ref[:, parts * BIN_DEV :, :] = fold.reshape(NU, BIN_DEV, LANES)


def finish_kernel(arrived_ref, out_ref):
    total = arrived_ref[0]
    for u in range(1, NU):
        total = total + arrived_ref[u]
    parts = total.shape[0] // BIN_DEV - 1
    scale = jnp.sqrt(jnp.maximum(total[parts * BIN_DEV :, :], 1.0))
    for c in range(parts):
        out_ref[:, c * LANES : (c + 1) * LANES] = total[c * BIN_DEV : (c + 1) * BIN_DEV, :] / scale


VMEM = pl.BlockSpec(memory_space=pltpu.VMEM)
ANY = pl.BlockSpec(memory_space=pl.ANY)
LIMIT = 24 * 1024 * 1024


def f32(*shape):
    return jax.ShapeDtypeStruct(shape, jnp.float32)


def correct(filters, code, traces, sample_map, before, after):
    rows, width = traces.shape
    taps = before.shape[1]
    length = (width // LANES) * SLOTS + BIN_DEV
    return pl.pallas_call(
        correct_kernel,
        out_shape=f32(PEERS, length, LANES),
        in_specs=[VMEM, VMEM, ANY, ANY, VMEM, VMEM],
        out_specs=ANY,
        scratch_shapes=[
            pltpu.VMEM((rows, width), jnp.float32),
            pltpu.VMEM((rows, width), jnp.int32),
            pltpu.VMEM((PEERS, length, LANES), jnp.float32),
            pltpu.SemaphoreType.DMA((4,)),
            pltpu.SemaphoreType.DMA((width // taps + 1,)),
        ],
        name="correct",
        compiler_params=pltpu.CompilerParams(vmem_limit_bytes=55000 * 1024),
    )(filters, code, traces, sample_map, before, after)


def on_vmem(kernel, shape, name, operand):
    return pl.pallas_call(
        kernel,
        out_shape=f32(*shape),
        in_specs=[VMEM],
        out_specs=VMEM,
        name=name,
        compiler_params=pltpu.CompilerParams(vmem_limit_bytes=LIMIT),
    )(operand)


def passed_along(value, axis, steps):
    count = lax.axis_size(axis)
    leading, last = (max(0, -steps), min(count, count - steps))
    return lax.ppermute(value, axis, [(source, source + steps) for source in range(leading, last)])


def per_device(traces, filters, owners, sub_bins, sample_map):
    rows, width = traces.shape
    taps = filters.shape[1]
    before = passed_along(traces[:, width - taps :], "section", 1)
    after = passed_along(traces[:, :taps], "section", -1)
    code = owners.reshape(1, rows) * BIN_DEV + sub_bins.reshape(1, rows)
    padded = jnp.pad(filters, ((0, 0), (0, taps)))
    sent = correct(padded, code, traces, sample_map, before, after)
    near = lax.all_to_all(sent, NEAR, split_axis=0, concat_axis=0, tiled=True)
    summed = on_vmem(combine_kernel, (NU, (width // LANES + 1) * BIN_DEV, LANES), "combine", near)
    arrived = lax.all_to_all(summed, "u", split_axis=0, concat_axis=0, tiled=True)
    return on_vmem(finish_kernel, (BIN_DEV, width), "finish", arrived)


def solution(mesh):
    fine = Mesh(mesh.devices.reshape(mesh.devices.shape[0], NY, NU, NW, NC), ("section",) + BINS)
    in_specs = (
        P(BINS, "section"),
        P(BINS, None),
        P(BINS, None),
        P(BINS),
        P(BINS, "section"),
    )
    return jax.shard_map(
        per_device, mesh=fine, in_specs=in_specs, out_specs=P(BINS, "section"), check_vma=False
    )
```

time: 75.7 us -> 75.5 us (level)
  the two profiles are of different devices: /device:TPU:2 before, /device:TPU:6 now
where the time goes in v3:
time: 75.5 us; the launch traced here: 75.2 us
  blocking collectives  60.3 us (80%)
  Pallas kernels  5.09 us (7%)
  starting transfers between devices  4.03 us (5%)
  waiting for transfers between devices  3.5 us (5%)
  local copies, waits for them, and re-layouts  1.56 us (2%)
    all_to_all x1, blocking collectives, per_device(): lax.all_to_all(summed, 'u', split_axis=0, concat_axis=0, tiled=True)  37.1 us
    all_to_all x1, blocking collectives, per_device(): near = lax.all_to_all(sent, NEAR, split_axis=0, concat_axis=0, tiled=True)  23.1 us
    pallas_call x1, Pallas kernels, correct(): pl.pallas_call(correct_kernel, out_shape=f32(PEERS, length, LANES), in_sp...  4.1 us
    ppermute x2, starting transfers between devices, passed_along(): lax.ppermute(value, axis, [(source, source + steps) for source in range(l...  4.03 us
    ppermute x2, waiting for transfers between devices, passed_along(): lax.ppermute(value, axis, [(source, source + steps) for source in range(l...  3.5 us
  transfers between devices with their start and end apart: 2, of which 1 were waited for; matrix products, arithmetic and copies ran while one was open for 2% of the time, Pallas kernels for 0%

profile of v3, /device:TPU:6, one launch (start us, length us, event | category | flops | bytes accessed | tf_op | source)
XLA Modules:
  0.0 75.2 jit_solution(10289246659652621138)
XLA Ops:
  0.0 0.9 %fusion.1 = (f32[64,256]{1,0:T(8,128)S(1)}, f32[64,256]{1,0:T(8,128)S(1)}) fusion(f32[64,1024]{1,0:T(8,128)} %traces_hbm.1), kind=kLoop, calls=%fused_computation.2 | loop fusion | bytes 262144 | tf_op jit(solution)/shard_map/slice | solution.py:219
  0.9 2.7 %collective-permute-start.1 = (f32[64,256]{1,0:T(8,128)S(1)}, f32[64,256]{1,0:T(8,128)S(1)}, u32[]{:S(2)}, u32[]{:S(2)}) collective-permute-start(f32[64,256]{1,0:T(8,128)S(1)} %get-tuple-element.5), channel_id=1, source_target_pairs={{128,0},{256,128},{384,256},{129,1},{257,129},{385,257},{130,2},{2... | collective-permute-start | bytes 196616 | tf_op jit(solution)/shard_map/ppermute | solution.py:212
  3.6 1.3 %collective-permute-start = (f32[64,256]{1,0:T(8,128)S(1)}, f32[64,256]{1,0:T(8,128)S(1)}, u32[]{:S(2)}, u32[]{:S(2)}) collective-permute-start(f32[64,256]{1,0:T(8,128)S(1)} %get-tuple-element.6), channel_id=1, source_target_pairs={{0,128},{128,256},{256,384},{1,129},{129,257},{257,385},{2,130},{1... | collective-permute-start | bytes 196616 | tf_op jit(solution)/shard_map/ppermute | solution.py:212
  4.9 0.7 fusion.code_ref
  5.6 0.7 pad.4.filter_ref
  6.3 0.0 collective-permute-done.1.after_ref
  6.3 3.5 %collective-permute-done.before_ref = f32[64,256]{1,0:T(8,128)S(1)} collective-permute-done((f32[64,256]{1,0:T(8,128)S(1)}, f32[64,256]{1,0:T(8,128)S(1)}, u32[]{:S(2)}, u32[]{:S(2)}) %collective-permute-start) | collective-permute-done | bytes 65568 | tf_op jit(solution)/shard_map/ppermute | solution.py:212
  9.8 4.1 %correct.1 = f32[16,136,128]{2,1,0:T(8,128)} custom-call(f32[1,512]{1,0:T(1,128)S(1)} %pad.4.filter_ref, s32[1,64]{1,0:T(1,128)S(1)} %fusion.code_ref, f32[64,1024]{1,0:T(8,128)} %traces_hbm.1, s32[64,1024]{1,0:T(8,128)} %map_hbm.1, f32[64,256]{1,0:T(8,128)S(1)} %collective-permute-done.before_ref, f32[64,256]{1,0:T(8,128)S(1)} %collective-permute-done.1.after_ref), custom_call_target="tpu_custom_call" | custom-call | tf_op jit(solution)/shard_map/correct/pallas_call | solution.py:181
  13.9 23.1 %all_to_all.10.arrived_ref = f32[16,136,128]{2,1,0:T(8,128)S(1)} all-to-all(f32[16,136,128]{2,1,0:T(8,128)} %correct.1), channel_id=1, replica_groups=mesh['section'=4,'y'=4,'u'=8,'w'=2,'c'=2] {'y','w','c'}, dimensions={0} | all-to-all | bytes 2228224 | tf_op jit(solution)/shard_map/all_to_all | solution.py:223
  37.0 0.4 combine.1
  37.4 37.1 %all_to_all.11.arrived_ref = f32[8,72,128]{2,1,0:T(8,128)S(1)} all-to-all(f32[8,72,128]{2,1,0:T(8,128)S(1)} %combine.1), channel_id=1, replica_groups=mesh['section'=4,'y'=4,'u'=8,'w'=2,'c'=2] {'u'}, dimensions={0} | all-to-all | bytes 589824 | tf_op jit(solution)/shard_map/all_to_all | solution.py:225
  74.5 0.6 finish.1
Async XLA Ops:
  0.9 5.4 %collective-permute-start.1 = (f32[64,256]{1,0:T(8,128)S(1)}, f32[64,256]{1,0:T(8,128)S(1)}, u32[]{:S(2)}, u32[]{:S(2)}) collective-permute-start(f32[64,256]{1,0:T(8,128)S(1)} %get-tuple-element.5), channel_id=1, source_target_pairs={{128,0},{256,128},{384,256},{129,1},{257,129},{385,257},{130,2},{2... | collective-permute-start | bytes 196616 | tf_op jit(solution)/shard_map/ppermute | solution.py:212
  3.6 6.2 %collective-permute-start = (f32[64,256]{1,0:T(8,128)S(1)}, f32[64,256]{1,0:T(8,128)S(1)}, u32[]{:S(2)}, u32[]{:S(2)}) collective-permute-start(f32[64,256]{1,0:T(8,128)S(1)} %get-tuple-element.6), channel_id=1, source_target_pairs={{0,128},{128,256},{256,384},{1,129},{129,257},{257,385},{2,130},{1... | collective-permute-start | bytes 196616 | tf_op jit(solution)/shard_map/ppermute | solution.py:212

commit v4 on v3

v4 whole, which is shorter than its diff:
```python
import jax
import jax.numpy as jnp
from jax import lax
from jax.experimental import pallas as pl
from jax.experimental.pallas import tpu as pltpu
from jax.sharding import Mesh
from jax.sharding import PartitionSpec as P

BIN_DEV = 8
CAP = 2
LANES = 128
NY, NU, NW, NC = 4, 8, 2, 2
BINS = ("y", "u", "w", "c")
NEAR = ("y", "w", "c")
PEERS = NY * NW * NC
SLOTS = NU * CAP
SHELVES = LANES // SLOTS


def halves(value):
    high = value.astype(jnp.bfloat16)
    low = (value - high.astype(jnp.float32)).astype(jnp.bfloat16)
    return high, low


def dot(a, b):
    return jnp.dot(a, b, preferred_element_type=jnp.float32)


def dot_split(a, b):
    return dot(a[0], b[0]) + (dot(a[1], b[0]) + dot(a[0], b[1]))


def move_out(window, quarters):
    rows, span = window.shape
    step = pltpu.roll(window, span - 1, 1) - window
    lane = lax.broadcasted_iota(jnp.int32, (rows, LANES), 1)
    moved = []
    for c, quarter in enumerate(quarters):
        place = lane + (quarter >> 2)
        weight = (quarter & 3).astype(jnp.float32) * 0.25
        inside = place & (LANES - 1)
        block = place >> 7
        near = slope = None
        for k in range(3):
            columns = slice((c + k) * LANES, (c + k + 1) * LANES)
            value = jnp.take_along_axis(window[:, columns], inside, axis=1, mode="promise_in_bounds")
            change = jnp.take_along_axis(step[:, columns], inside, axis=1, mode="promise_in_bounds")
            near = value if k == 0 else jnp.where(block == k, value, near)
            slope = change if k == 0 else jnp.where(block == k, change, slope)
        moved.append(near + weight * slope)
    return jnp.concatenate(moved, axis=1)


def place_slots(slot, moved):
    number = lax.broadcasted_iota(jnp.int32, (PEERS * SLOTS, moved.shape[0]), 0)
    member = jnp.where(number == slot, 1.0, 0.0).astype(jnp.bfloat16)
    high, low = halves(moved)
    return dot(member, high) + dot(member, low)


def inner_kernel(
    filter_ref, code_ref, traces_hbm, map_hbm,
    high_ref, low_ref, edge_ref, edge_map_ref, slot_ref, label_ref, *rest,
):
    *placed_refs, traces_ref, map_ref, sems = rest
    rows, width = traces_ref.shape
    taps = filter_ref.shape[1] // 2
    half = width // 2
    count = width // taps
    loads = []
    for part in range(2):
        columns = pl.ds(part * half, half)
        loads.append(pltpu.make_async_copy(traces_hbm.at[:, columns], traces_ref.at[:, columns], sems.at[part]))
    loads += [
        pltpu.make_async_copy(map_hbm.at[:, taps : taps + half], map_ref, sems.at[2]),
        pltpu.make_async_copy(map_hbm.at[:, :taps], edge_map_ref.at[:, :taps], sems.at[3]),
        pltpu.make_async_copy(map_hbm.at[:, taps + half :], edge_map_ref.at[:, taps:], sems.at[4]),
    ]
    for load in loads:
        load.start()
    shifted = pltpu.roll(jnp.broadcast_to(filter_ref[...], (taps, 2 * taps)), 0, 1, stride=1, stride_axis=0)
    toeplitz = halves(shifted)
    high_ref[...], low_ref[...] = toeplitz

    owner = code_ref[...] // BIN_DEV
    sub = code_ref[...] % BIN_DEV
    owners = NY * NU * NW * NC
    named = lax.broadcasted_iota(jnp.int32, (owners, rows), 0) == owner
    named = jnp.where(named, 1.0, 0.0)
    earlier = lax.broadcasted_iota(jnp.int32, (rows, rows), 0) < lax.broadcasted_iota(jnp.int32, (rows, rows), 1)
    earlier = jnp.where(earlier, 1.0, 0.0).astype(jnp.bfloat16)
    rank = jnp.sum(named * dot(named.astype(jnp.bfloat16), earlier), axis=0, keepdims=True).astype(jnp.int32)
    core, w = owner % NC, owner // NC % NW
    u, y = owner // (NC * NW) % NU, owner // (NC * NW * NU)
    peer = (y * NW + w) * NC + core
    within = u * CAP + rank
    slot = peer * SLOTS + within
    slot_ref[...] = slot
    to_peer = lax.broadcasted_iota(jnp.int32, (PEERS, rows), 0) == peer
    to_peer = jnp.where(to_peer, (sub + 1).astype(jnp.float32), 0.0).astype(jnp.bfloat16)
    column = lax.broadcasted_iota(jnp.int32, (LANES, rows), 0)
    shelf = lax.rem(lax.axis_index(NEAR), SHELVES) * SLOTS
    in_column = jnp.where(column == within + shelf, 1.0, 0.0).astype(jnp.bfloat16)
    label_ref[...] = lax.dot_general(
        to_peer, in_column, (((1,), (1,)), ((), ())), preferred_element_type=jnp.float32
    )

    loads[0].wait()
    loads[1].wait()
    stacked = jnp.concatenate([traces_ref[:, b * taps : (b + 1) * taps] for b in range(count)], axis=0)
    spread = dot_split(halves(stacked), toeplitz)
    pieces = [
        spread[b * rows : (b + 1) * rows, :taps] + spread[(b - 1) * rows : b * rows, taps:] for b in range(1, count)
    ]
    edge_ref[:, :taps] = spread[:rows, :taps]
    edge_ref[:, taps : 2 * taps] = pieces[0]
    edge_ref[:, 2 * taps : 3 * taps] = pieces[-1]
    edge_ref[:, 3 * taps :] = spread[(count - 1) * rows :, taps:]
    loads[2].wait()
    quarters = [map_ref[:, c * LANES : (c + 1) * LANES] for c in range(half // LANES)]
    placed = place_slots(slot, move_out(jnp.concatenate(pieces, axis=1), quarters))
    for c, placed_ref in enumerate(placed_refs):
        placed_ref[...] = placed[:, c * LANES : (c + 1) * LANES]
    loads[3].wait()
    loads[4].wait()


def outer_kernel(before_ref, after_ref, high_ref, low_ref, edge_ref, edge_map_ref, slot_ref, label_ref, *rest):
    *placed_refs, out_ref = rest
    taps = before_ref.shape[1]
    parts = taps // LANES
    length = out_ref.shape[0] // PEERS
    slot = slot_ref[...]

    def put(c, placed):
        for peer in range(PEERS):
            start = peer * length + c * SLOTS
            out_ref[start : start + SLOTS, :] = placed[peer * SLOTS : (peer + 1) * SLOTS, :]

    def put_edge(c, k, window):
        quarters = [edge_map_ref[:, (k + i) * LANES : (k + i + 1) * LANES] for i in range(parts)]
        placed = place_slots(slot, move_out(window, quarters))
        for i in range(parts):
            put(c + i, placed[:, i * LANES : (i + 1) * LANES])

    early = dot_split(halves(before_ref[...]), (high_ref[:, taps:], low_ref[:, taps:])) + edge_ref[:, :taps]
    put_edge(0, 0, jnp.concatenate([early, edge_ref[:, taps : 2 * taps]], axis=1))
    late = dot_split(halves(after_ref[...]), (high_ref[:, :taps], low_ref[:, :taps])) + edge_ref[:, 3 * taps :]
    late = jnp.where(lax.axis_index("section") == lax.axis_size("section") - 1, 0.0, late)
    put_edge(parts + len(placed_refs), parts, jnp.concatenate([edge_ref[:, 2 * taps : 3 * taps], late], axis=1))
    for c, placed_ref in enumerate(placed_refs):
        put(parts + c, placed_ref)
    for peer in range(PEERS):
        out_ref[(peer + 1) * length - 1 : (peer + 1) * length, :] = label_ref[peer : peer + 1, :]


def combine_kernel(arrived_ref, out_ref):
    length = arrived_ref.shape[0] // PEERS
    out_length = out_ref.shape[0] // NU
    parts = length // SLOTS
    shelves = []
    for first in range(0, PEERS, SHELVES):
        row = sum(arrived_ref[(peer + 1) * length - 1 : (peer + 1) * length, :] for peer in range(first, first + SHELVES))
        shelves.append(row)
    labels = jnp.concatenate(shelves, axis=1)
    slots = PEERS * SLOTS
    shape = (NU * BIN_DEV, slots)
    row = lax.broadcasted_iota(jnp.int32, shape, 0)
    column = lax.broadcasted_iota(jnp.int32, shape, 1)
    bin_label = (row % BIN_DEV + 1).astype(jnp.float32)
    hit = (labels == bin_label) & (row // BIN_DEV == column % SLOTS // CAP)
    member = jnp.where(hit, 1.0, 0.0).astype(jnp.bfloat16)
    for c in range(0, parts, 2):
        pair = []
        for k in (c, c + 1):
            starts = [peer * length + k * SLOTS for peer in range(PEERS)]
            pair.append(jnp.concatenate([arrived_ref[start : start + SLOTS, :] for start in starts], axis=0))
        high, low = halves(jnp.concatenate(pair, axis=1))
        total = dot(member, high) + dot(member, low)
        for k in (0, 1):
            for u in range(NU):
                start = u * out_length + (c + k) * BIN_DEV
                out_ref[start : start + BIN_DEV, :] = total[
                    u * BIN_DEV : (u + 1) * BIN_DEV, k * LANES : (k + 1) * LANES
                ]
    column = lax.broadcasted_iota(jnp.int32, (NU, slots), 1)
    of_owner = (lax.broadcasted_iota(jnp.int32, (NU, slots), 0) == column % SLOTS // CAP) & (labels > 0.0)
    of_owner = jnp.where(of_owner, 1.0, 0.0).astype(jnp.bfloat16)
    of_bin = labels == (lax.broadcasted_iota(jnp.int32, (LANES, slots), 0) + 1).astype(jnp.float32)
    of_bin = jnp.where(of_bin, 1.0, 0.0).astype(jnp.bfloat16)
    fold = lax.dot_general(of_owner, of_bin, (((1,), (1,)), ((), ())), preferred_element_type=jnp.float32)
    for u in range(NU):
        out_ref[(u + 1) * out_length - 1 : (u + 1) * out_length, :] = fold[u : u + 1, :]


def finish_kernel(arrived_ref, out_ref):
    length = arrived_ref.shape[0] // NU
    fold = sum(arrived_ref[(u + 1) * length - 1 : (u + 1) * length, :] for u in range(NU))
    diagonal = lax.broadcasted_iota(jnp.int32, (BIN_DEV, LANES), 0) == lax.broadcasted_iota(jnp.int32, (BIN_DEV, LANES), 1)
    counts = jnp.sum(jnp.where(diagonal, fold, 0.0), axis=1, keepdims=True)
    scale = jnp.sqrt(jnp.maximum(counts, 1.0))
    for c in range(length // BIN_DEV):
        starts = [u * length + c * BIN_DEV for u in range(NU)]
        total = sum(arrived_ref[start : start + BIN_DEV, :] for start in starts)
        out_ref[:, c * LANES : (c + 1) * LANES] = total / scale


VMEM = pl.BlockSpec(memory_space=pltpu.VMEM)
ANY = pl.BlockSpec(memory_space=pl.ANY)
LIMIT = 24 * 1024 * 1024
INNER_LIMIT = 53760


def f32(*shape):
    return jax.ShapeDtypeStruct(shape, jnp.float32)


def correct_inner(filters, code, traces, sample_map):
    rows, width = traces.shape
    taps = filters.shape[1] // 2
    inner = (width - 2 * taps) // LANES
    return pl.pallas_call(
        inner_kernel,
        out_shape=(
            jax.ShapeDtypeStruct((taps, 2 * taps), jnp.bfloat16),
            jax.ShapeDtypeStruct((taps, 2 * taps), jnp.bfloat16),
            f32(rows, 4 * taps),
            jax.ShapeDtypeStruct((rows, 2 * taps), jnp.int32),
            jax.ShapeDtypeStruct((1, rows), jnp.int32),
            f32(PEERS, LANES),
        )
        + (f32(PEERS * SLOTS, LANES),) * inner,
        in_specs=[VMEM, VMEM, ANY, ANY],
        out_specs=(VMEM,) * (6 + inner),
        scratch_shapes=[
            pltpu.VMEM((rows, width), jnp.float32),
            pltpu.VMEM((rows, inner * LANES), jnp.int32),
            pltpu.SemaphoreType.DMA((5,)),
        ],
        name="correct_inner",
        cost_estimate=pl.CostEstimate(flops=500_000_000, bytes_accessed=2_000_000, transcendentals=0),
        compiler_params=pltpu.CompilerParams(vmem_limit_bytes=INNER_LIMIT * 1024),
    )(filters, code, traces, sample_map)


def on_vmem(kernel, shape, name, *operands):
    return pl.pallas_call(
        kernel,
        out_shape=f32(*shape),
        in_specs=[VMEM] * len(operands),
        out_specs=VMEM,
        name=name,
        compiler_params=pltpu.CompilerParams(vmem_limit_bytes=LIMIT),
    )(*operands)


def passed_along(value, axis, steps):
    count = lax.axis_size(axis)
    leading, last = (max(0, -steps), min(count, count - steps))
    return lax.ppermute(value, axis, [(source, source + steps) for source in range(leading, last)])


def exchanged(rows, axes):
    count, lanes = rows.shape
    sent = rows.reshape(count, 1, lanes)
    return lax.all_to_all(sent, axes, split_axis=0, concat_axis=0, tiled=True).reshape(count, lanes)


def per_device(traces, filters, owners, sub_bins, sample_map):
    rows, width = traces.shape
    taps = filters.shape[1]
    before = passed_along(traces[:, width - taps :], "section", 1)
    after = passed_along(traces[:, :taps], "section", -1)
    code = owners.reshape(1, rows) * BIN_DEV + sub_bins.reshape(1, rows)
    padded = jnp.pad(filters, ((0, 0), (0, taps)))
    kept = correct_inner(padded, code, traces, sample_map)
    parts = width // LANES
    sent = on_vmem(outer_kernel, (PEERS * (parts * SLOTS + 1), LANES), "correct_outer", before, after, *kept)
    near = exchanged(sent, NEAR)
    summed = on_vmem(combine_kernel, (NU * (parts * BIN_DEV + 1), LANES), "combine", near)
    arrived = exchanged(summed, "u")
    return on_vmem(finish_kernel, (BIN_DEV, width), "finish", arrived)


def solution(mesh):
    fine = Mesh(mesh.devices.reshape(mesh.devices.shape[0], NY, NU, NW, NC), ("section",) + BINS)
    in_specs = (
        P(BINS, "section"),
        P(BINS, None),
        P(BINS, None),
        P(BINS),
        P(BINS, "section"),
    )
    return jax.shard_map(
        per_device, mesh=fine, in_specs=in_specs, out_specs=P(BINS, "section"), check_vma=False
    )
```

time: 75.5 us -> 71.6 us (0.948); the launches traced: 75.2 us -> 70.3 us
  waiting for transfers between devices: 3.5 us -> 0.85 us
  blocking collectives: 60.3 us -> 58.2 us
    ppermute x2, waiting for transfers between devices: 3.5 us -> 0.85 us  [passed_along(): lax.ppermute(value, axis, [(source, source + steps) for source in range(l...]
    all_to_all x2, blocking collectives: 60.3 us -> 58.2 us  [exchanged(): lax.all_to_all(sent, axes, split_axis=0, concat_axis=0, tiled=True)]
    pallas_call x3 -> x4, Pallas kernels: 5.09 us -> 4.93 us  [the longest x1 2.63 us: correct_inner(): pl.pallas_call(inner_kernel, out_shape=(jax.ShapeDtypeStruct((taps, 2 * t...]
  transfers between devices with their start and end apart: 2 -> 2, of which waited for: 1 -> 1; matrix products, arithmetic and copies ran while one was open for 2% -> 2% of each run, Pallas kernels for 0% -> 4%
where the time goes in v4:
time: 71.6 us; the launch traced here: 70.3 us
  blocking collectives  58.2 us (81%)
  Pallas kernels  4.93 us (7%)
  starting transfers between devices  4.03 us (6%)
  local copies, waits for them, and re-layouts  1.56 us (2%)
  waiting for transfers between devices  0.85 us (1%)
    all_to_all x2, blocking collectives, exchanged(): lax.all_to_all(sent, axes, split_axis=0, concat_axis=0, tiled=True)  58.2 us
    ppermute x2, starting transfers between devices, passed_along(): lax.ppermute(value, axis, [(source, source + steps) for source in range(l...  4.03 us
    pallas_call x1, Pallas kernels, correct_inner(): pl.pallas_call(inner_kernel, out_shape=(jax.ShapeDtypeStruct((taps, 2 * t...  2.63 us
    pallas_call x3, Pallas kernels, on_vmem(): pl.pallas_call(kernel, out_shape=f32(*shape), in_specs=[VMEM] * len(opera...  2.3 us
  transfers between devices with their start and end apart: 2, of which 1 were waited for; matrix products, arithmetic and copies ran while one was open for 2% of the time, Pallas kernels for 4%

profile of v4, /device:TPU:6, one launch (start us, length us, event | category | flops | bytes accessed | tf_op | source)
XLA Modules:
  0.0 70.3 jit_solution(16507420762589038772)
XLA Ops:
  0.0 0.9 %fusion.1 = (f32[64,256]{1,0:T(8,128)S(1)}, f32[64,256]{1,0:T(8,128)S(1)}) fusion(f32[64,1024]{1,0:T(8,128)} %traces_hbm.1), kind=kLoop, calls=%fused_computation.2 | loop fusion | bytes 262144 | tf_op jit(solution)/shard_map/slice | solution.py:274
  0.9 2.7 %collective-permute-start.1 = (f32[64,256]{1,0:T(8,128)S(1)}, f32[64,256]{1,0:T(8,128)S(1)}, u32[]{:S(2)}, u32[]{:S(2)}) collective-permute-start(f32[64,256]{1,0:T(8,128)S(1)} %get-tuple-element.25), channel_id=1, source_target_pairs={{128,0},{256,128},{384,256},{129,1},{257,129},{385,257},{130,2},{2... | collective-permute-start | bytes 196616 | tf_op jit(solution)/shard_map/ppermute | solution.py:261
  3.6 1.3 %collective-permute-start = (f32[64,256]{1,0:T(8,128)S(1)}, f32[64,256]{1,0:T(8,128)S(1)}, u32[]{:S(2)}, u32[]{:S(2)}) collective-permute-start(f32[64,256]{1,0:T(8,128)S(1)} %get-tuple-element.26), channel_id=1, source_target_pairs={{0,128},{128,256},{256,384},{1,129},{129,257},{257,385},{2,130},{1... | collective-permute-start | bytes 196616 | tf_op jit(solution)/shard_map/ppermute | solution.py:261
  4.9 0.7 fusion.code_ref
  5.6 0.7 pad.4.filter_ref
  6.3 2.6 %correct_inner.1 = (bf16[256,512]{1,0:T(8,128)(2,1)S(1)}, bf16[256,512]{1,0:T(8,128)(2,1)S(1)}, f32[64,1024]{1,0:T(8,128)S(1)}, s32[64,512]{1,0:T(8,128)S(1)}, s...) custom-call(f32[1,512]{1,0:T(1,128)S(1)} %pad.4.filter_ref, ...), custom_call_target="tpu_custom_call" | custom-call | flops 500000000 | bytes 2000000 | tf_op jit(solution)/shard_map/correct_inner/pallas_call | solution.py:223
  8.9 0.0 collective-permute-done.1.after_ref
  8.9 0.8 %collective-permute-done.before_ref = f32[64,256]{1,0:T(8,128)S(1)} collective-permute-done((f32[64,256]{1,0:T(8,128)S(1)}, f32[64,256]{1,0:T(8,128)S(1)}, u32[]{:S(2)}, u32[]{:S(2)}) %collective-permute-start) | collective-permute-done | bytes 65568 | tf_op jit(solution)/shard_map/ppermute | solution.py:261
  9.8 1.2 %correct_outer.1 = f32[2064,128]{1,0:T(8,128)S(1)} custom-call(f32[64,256]{1,0:T(8,128)S(1)} %collective-permute-done.before_ref, f32[64,256]{1,0:T(8,128)S(1)} %collective-permute-done.1.after_ref, bf16[256,512]{1,0:T(8,128)(2,1)S(1)} %get-tuple-element.15.high_ref, bf16[256,512]{1,0:T(8,128)(2,1)S(1)} %get-tuple-element.16.low_ref, ...), custom_call_target="tpu_custom_call" | custom-call | tf_op jit(solution)/shard_map/correct_outer/pallas_call | solution.py:248
  11.0 22.5 %all_to_all.10 = f32[2064,1,128]{2,1,0:T(1,128)S(1)} all-to-all(f32[2064,1,128]{2,1,0:T(1,128)S(1)} %bitcast.14), channel_id=1, replica_groups=mesh['section'=4,'y'=4,'u'=8,'w'=2,'c'=2] {'y','w','c'}, dimensions={0} | all-to-all | bytes 2113536 | tf_op jit(solution)/shard_map/all_to_all | solution.py:267
  33.5 0.4 combine.1
  33.9 35.7 %all_to_all.11 = f32[520,1,128]{2,1,0:T(1,128)S(1)} all-to-all(f32[520,1,128]{2,1,0:T(1,128)S(1)} %bitcast.16), channel_id=1, replica_groups=mesh['section'=4,'y'=4,'u'=8,'w'=2,'c'=2] {'u'}, dimensions={0} | all-to-all | bytes 532480 | tf_op jit(solution)/shard_map/all_to_all | solution.py:267
  69.6 0.7 %finish.1 = f32[8,1024]{1,0:T(8,128)} custom-call(f32[520,128]{1,0:T(8,128)S(1)} %bitcast.17), custom_call_target="tpu_custom_call" | custom-call | tf_op jit(solution)/shard_map/finish/pallas_call | solution.py:248
Async XLA Ops:
  0.9 8.0 %collective-permute-start.1 = (f32[64,256]{1,0:T(8,128)S(1)}, f32[64,256]{1,0:T(8,128)S(1)}, u32[]{:S(2)}, u32[]{:S(2)}) collective-permute-start(f32[64,256]{1,0:T(8,128)S(1)} %get-tuple-element.25), channel_id=1, source_target_pairs={{128,0},{256,128},{384,256},{129,1},{257,129},{385,257},{130,2},{2... | collective-permute-start | bytes 196616 | tf_op jit(solution)/shard_map/ppermute | solution.py:261
  3.6 6.2 %collective-permute-start = (f32[64,256]{1,0:T(8,128)S(1)}, f32[64,256]{1,0:T(8,128)S(1)}, u32[]{:S(2)}, u32[]{:S(2)}) collective-permute-start(f32[64,256]{1,0:T(8,128)S(1)} %get-tuple-element.26), channel_id=1, source_target_pairs={{0,128},{128,256},{256,384},{1,129},{129,257},{257,385},{2,130},{1... | collective-permute-start | bytes 196616 | tf_op jit(solution)/shard_map/ppermute | solution.py:261

commit v5 on v4

--- a/solution.py
+++ b/solution.py
@@ -60,12 +60,12 @@
 
 
 def inner_kernel(
-    filter_ref, code_ref, traces_hbm, map_hbm,
+    small_ref, traces_hbm, map_hbm,
     high_ref, low_ref, edge_ref, edge_map_ref, slot_ref, label_ref, *rest,
 ):
     *placed_refs, traces_ref, map_ref, sems = rest
     rows, width = traces_ref.shape
-    taps = filter_ref.shape[1] // 2
+    taps = (small_ref.shape[1] - LANES) // 2
     half = width // 2
     count = width // taps
     loads = []
@@ -79,12 +79,12 @@
     ]
     for load in loads:
         load.start()
-    shifted = pltpu.roll(jnp.broadcast_to(filter_ref[...], (taps, 2 * taps)), 0, 1, stride=1, stride_axis=0)
+    shifted = pltpu.roll(jnp.broadcast_to(small_ref[:, : 2 * taps], (taps, 2 * taps)), 0, 1, stride=1, stride_axis=0)
     toeplitz = halves(shifted)
     high_ref[...], low_ref[...] = toeplitz
 
-    owner = code_ref[...] // BIN_DEV
-    sub = code_ref[...] % BIN_DEV
+    code = small_ref[:, 2 * taps : 2 * taps + rows].astype(jnp.int32)
+    owner, sub = code // BIN_DEV, code % BIN_DEV
     owners = NY * NU * NW * NC
     named = lax.broadcasted_iota(jnp.int32, (owners, rows), 0) == owner
     named = jnp.where(named, 1.0, 0.0)
@@ -126,9 +126,9 @@
     loads[4].wait()
 
 
-def outer_kernel(before_ref, after_ref, high_ref, low_ref, edge_ref, edge_map_ref, slot_ref, label_ref, *rest):
+def outer_kernel(pair_ref, cross_ref, high_ref, low_ref, edge_ref, edge_map_ref, slot_ref, label_ref, *rest):
     *placed_refs, out_ref = rest
-    taps = before_ref.shape[1]
+    taps = pair_ref.shape[1]
     parts = taps // LANES
     length = out_ref.shape[0] // PEERS
     slot = slot_ref[...]
@@ -144,10 +144,14 @@
         for i in range(parts):
             put(c + i, placed[:, i * LANES : (i + 1) * LANES])
 
-    early = dot_split(halves(before_ref[...]), (high_ref[:, taps:], low_ref[:, taps:])) + edge_ref[:, :taps]
+    place = lax.axis_index("section")
+    odd = lax.rem(place, 2) == 1
+    pair, cross = pair_ref[...], cross_ref[...]
+    before, after = jnp.where(odd, pair, cross), jnp.where(odd, cross, pair)
+    early = dot_split(halves(before), (high_ref[:, taps:], low_ref[:, taps:])) + edge_ref[:, :taps]
     put_edge(0, 0, jnp.concatenate([early, edge_ref[:, taps : 2 * taps]], axis=1))
-    late = dot_split(halves(after_ref[...]), (high_ref[:, :taps], low_ref[:, :taps])) + edge_ref[:, 3 * taps :]
-    late = jnp.where(lax.axis_index("section") == lax.axis_size("section") - 1, 0.0, late)
+    late = dot_split(halves(after), (high_ref[:, :taps], low_ref[:, :taps])) + edge_ref[:, 3 * taps :]
+    late = jnp.where(place == lax.axis_size("section") - 1, 0.0, late)
     put_edge(parts + len(placed_refs), parts, jnp.concatenate([edge_ref[:, 2 * taps : 3 * taps], late], axis=1))
     for c, placed_ref in enumerate(placed_refs):
         put(parts + c, placed_ref)
@@ -216,9 +220,9 @@
     return jax.ShapeDtypeStruct(shape, jnp.float32)
 
 
-def correct_inner(filters, code, traces, sample_map):
+def correct_inner(small, traces, sample_map):
     rows, width = traces.shape
-    taps = filters.shape[1] // 2
+    taps = (small.shape[1] - LANES) // 2
     inner = (width - 2 * taps) // LANES
     return pl.pallas_call(
         inner_kernel,
@@ -231,7 +235,7 @@
             f32(PEERS, LANES),
         )
         + (f32(PEERS * SLOTS, LANES),) * inner,
-        in_specs=[VMEM, VMEM, ANY, ANY],
+        in_specs=[VMEM, ANY, ANY],
         out_specs=(VMEM,) * (6 + inner),
         scratch_shapes=[
             pltpu.VMEM((rows, width), jnp.float32),
@@ -241,7 +245,7 @@
         name="correct_inner",
         cost_estimate=pl.CostEstimate(flops=500_000_000, bytes_accessed=2_000_000, transcendentals=0),
         compiler_params=pltpu.CompilerParams(vmem_limit_bytes=INNER_LIMIT * 1024),
-    )(filters, code, traces, sample_map)
+    )(small, traces, sample_map)
 
 
 def on_vmem(kernel, shape, name, *operands):
@@ -255,10 +259,10 @@
     )(*operands)
 
 
-def passed_along(value, axis, steps):
+def swapped(value, axis, first):
     count = lax.axis_size(axis)
-    leading, last = (max(0, -steps), min(count, count - steps))
-    return lax.ppermute(value, axis, [(source, source + steps) for source in range(leading, last)])
+    pairs = [(one, one + 1) for one in range(first, count - 1, 2)]
+    return lax.ppermute(value, axis, pairs + [(other, one) for one, other in pairs])
 
 
 def exchanged(rows, axes):
@@ -270,13 +274,14 @@
 def per_device(traces, filters, owners, sub_bins, sample_map):
     rows, width = traces.shape
     taps = filters.shape[1]
-    before = passed_along(traces[:, width - taps :], "section", 1)
-    after = passed_along(traces[:, :taps], "section", -1)
-    code = owners.reshape(1, rows) * BIN_DEV + sub_bins.reshape(1, rows)
-    padded = jnp.pad(filters, ((0, 0), (0, taps)))
-    kept = correct_inner(padded, code, traces, sample_map)
+    odd = lax.axis_index("section") % 2
+    ends = [lax.dynamic_slice_in_dim(traces, (width - taps) * use_tail, taps, 1) for use_tail in (1 - odd, odd)]
+    pair, cross = swapped(ends[0], "section", 0), swapped(ends[1], "section", 1)
+    code = (owners.reshape(1, rows) * BIN_DEV + sub_bins.reshape(1, rows)).astype(jnp.float32)
+    small = jnp.pad(filters, ((0, 0), (0, taps + LANES))) + jnp.pad(code, ((0, 0), (2 * taps, LANES - rows)))
+    kept = correct_inner(small, traces, sample_map)
     parts = width // LANES
-    sent = on_vmem(outer_kernel, (PEERS * (parts * SLOTS + 1), LANES), "correct_outer", before, after, *kept)
+    sent = on_vmem(outer_kernel, (PEERS * (parts * SLOTS + 1), LANES), "correct_outer", pair, cross, *kept)
     near = exchanged(sent, NEAR)
     summed = on_vmem(combine_kernel, (NU * (parts * BIN_DEV + 1), LANES), "combine", near)
     arrived = exchanged(summed, "u")

time: 71.6 us -> 71.3 us (level)
  starting transfers between devices: 4.03 us -> 5.18 us
  waiting for transfers between devices: 0.85 us -> 0.01 us
    ppermute x2, starting transfers between devices: 4.03 us -> 5.18 us  [swapped(): lax.ppermute(value, axis, pairs + [(other, one) for one, other in pairs])]
    dynamic_slice x0 -> x1, local copies, waits for them, and re-layouts: none -> 0.88 us  [per_device(): lax.dynamic_slice_in_dim(traces, (width - taps) * use_tail, taps, 1)]
    slice x1 -> x0, local copies, waits for them, and re-layouts: 0.88 us -> none  [per_device(): after = passed_along(traces[:, :taps], 'section', -1)]
    ppermute x2, waiting for transfers between devices: 0.85 us -> 0.01 us  [swapped(): lax.ppermute(value, axis, pairs + [(other, one) for one, other in pairs])]
  transfers between devices with their start and end apart: 2 -> 2, of which waited for: 1 -> 0; matrix products, arithmetic and copies ran while one was open for 2% -> 2% of each run, Pallas kernels for 4% -> 4%
where the time goes in v5:
time: 71.3 us; the launch traced here: 70.6 us
  blocking collectives  58.2 us (82%)
  starting transfers between devices  5.18 us (7%)
  Pallas kernels  4.93 us (7%)
  other arithmetic  1.36 us (2%)
  local copies, waits for them, and re-layouts  0.88 us (1%)
    all_to_all x2, blocking collectives, exchanged(): lax.all_to_all(sent, axes, split_axis=0, concat_axis=0, tiled=True)  58.2 us
    ppermute x2, starting transfers between devices, swapped(): lax.ppermute(value, axis, pairs + [(other, one) for one, other in pairs])  5.18 us
    pallas_call x1, Pallas kernels, correct_inner(): pl.pallas_call(inner_kernel, out_shape=(jax.ShapeDtypeStruct((taps, 2 * t...  2.63 us
    pallas_call x3, Pallas kernels, on_vmem(): pl.pallas_call(kernel, out_shape=f32(*shape), in_specs=[VMEM] * len(opera...  2.3 us
  transfers between devices with their start and end apart: 2, of which 0 were waited for; matrix products, arithmetic and copies ran while one was open for 2% of the time, Pallas kernels for 4%

profile of v5, /device:TPU:6, one launch (start us, length us, event | category | flops | bytes accessed | tf_op | source)
XLA Modules:
  0.0 70.6 jit_solution(1458327303561154354)
XLA Ops:
  0.0 0.9 %constant_dynamic-slice_fusion = (f32[64,256]{1,0:T(8,128)S(1)}, f32[64,256]{1,0:T(8,128)S(1)}) fusion(f32[64,1024]{1,0:T(8,128)} %traces_hbm.1, s32[]{:T(128)S(6)} %select_n.15, s32[]{:T(128)S(6)} %select_n.14), kind=kLoop, calls=%fused_computation.4 | loop fusion | bytes 262152 | tf_op jit(solution)/shard_map/dynamic_slice | solution.py:278
  0.9 0.7 collective-permute-start.1
  1.6 4.5 %collective-permute-start = (f32[64,256]{1,0:T(8,128)S(1)}, f32[64,256]{1,0:T(8,128)S(1)}, u32[]{:S(2)}, u32[]{:S(2)}) collective-permute-start(f32[64,256]{1,0:T(8,128)S(1)} %get-tuple-element.26), channel_id=1, source_target_pairs={{0,128},{256,384},{128,0},{384,256},{1,129},{257,385},{129,1},{385... | collective-permute-start | bytes 196616 | tf_op jit(solution)/shard_map/ppermute | solution.py:265
  6.1 0.7 fusion.1
  6.8 0.7 pad_add_fusion.small_ref
  7.4 2.6 %correct_inner.1 = (bf16[256,512]{1,0:T(8,128)(2,1)S(1)}, bf16[256,512]{1,0:T(8,128)(2,1)S(1)}, f32[64,1024]{1,0:T(8,128)S(1)}, s32[64,512]{1,0:T(8,128)S(1)}, s...) custom-call(f32[1,640]{1,0:T(1,128)S(1)} %pad_add_fusion.small_ref, ...), custom_call_target="tpu_custom_call" | custom-call | flops 500000000 | bytes 2000000 | tf_op jit(solution)/shard_map/correct_inner/pallas_call | solution.py:227
  10.1 0.0 collective-permute-done.1.cross_ref
  10.1 0.0 collective-permute-done.pair_ref
  10.1 1.2 %correct_outer.1 = f32[2064,128]{1,0:T(8,128)S(1)} custom-call(f32[64,256]{1,0:T(8,128)S(1)} %collective-permute-done.pair_ref, f32[64,256]{1,0:T(8,128)S(1)} %collective-permute-done.1.cross_ref, bf16[256,512]{1,0:T(8,128)(2,1)S(1)} %get-tuple-element.15.high_ref, bf16[256,512]{1,0:T(8,128)(2,1)S(1)} %get-tuple-element.16.low_ref, ...), custom_call_target="tpu_custom_call" | custom-call | tf_op jit(solution)/shard_map/correct_outer/pallas_call | solution.py:252
  11.3 22.5 %all_to_all.10 = f32[2064,1,128]{2,1,0:T(1,128)S(1)} all-to-all(f32[2064,1,128]{2,1,0:T(1,128)S(1)} %bitcast.16), channel_id=1, replica_groups=mesh['section'=4,'y'=4,'u'=8,'w'=2,'c'=2] {'y','w','c'}, dimensions={0} | all-to-all | bytes 2113536 | tf_op jit(solution)/shard_map/all_to_all | solution.py:271
  33.9 0.4 combine.1
  34.2 35.7 %all_to_all.11 = f32[520,1,128]{2,1,0:T(1,128)S(1)} all-to-all(f32[520,1,128]{2,1,0:T(1,128)S(1)} %bitcast.18), channel_id=1, replica_groups=mesh['section'=4,'y'=4,'u'=8,'w'=2,'c'=2] {'u'}, dimensions={0} | all-to-all | bytes 532480 | tf_op jit(solution)/shard_map/all_to_all | solution.py:271
  69.9 0.7 %finish.1 = f32[8,1024]{1,0:T(8,128)} custom-call(f32[520,128]{1,0:T(8,128)S(1)} %bitcast.19), custom_call_target="tpu_custom_call" | custom-call | tf_op jit(solution)/shard_map/finish/pallas_call | solution.py:252
Async XLA Ops:
  0.9 9.2 %collective-permute-start.1 = (f32[64,256]{1,0:T(8,128)S(1)}, f32[64,256]{1,0:T(8,128)S(1)}, u32[]{:S(2)}, u32[]{:S(2)}) collective-permute-start(f32[64,256]{1,0:T(8,128)S(1)} %get-tuple-element.25), channel_id=1, source_target_pairs={{128,256},{256,128},{129,257},{257,129},{130,258},{258,130},{131,2... | collective-permute-start | bytes 196616 | tf_op jit(solution)/shard_map/ppermute | solution.py:265
  1.6 8.5 %collective-permute-start = (f32[64,256]{1,0:T(8,128)S(1)}, f32[64,256]{1,0:T(8,128)S(1)}, u32[]{:S(2)}, u32[]{:S(2)}) collective-permute-start(f32[64,256]{1,0:T(8,128)S(1)} %get-tuple-element.26), channel_id=1, source_target_pairs={{0,128},{256,384},{128,0},{384,256},{1,129},{257,385},{129,1},{385... | collective-permute-start | bytes 196616 | tf_op jit(solution)/shard_map/ppermute | solution.py:265

commit v6 on v5

--- a/solution.py
+++ b/solution.py
@@ -28,7 +28,11 @@
 
 
 def dot_split(a, b):
-    return dot(a[0], b[0]) + (dot(a[1], b[0]) + dot(a[0], b[1]))
+    return dot(jnp.concatenate([a[0], a[1], a[0]], axis=1), jnp.concatenate([b[0], b[0], b[1]], axis=0))
+
+
+def dot_exact(member, value):
+    return dot(jnp.concatenate([member, member], axis=1), jnp.concatenate(halves(value), axis=0))
 
 
 def move_out(window, quarters):
@@ -55,8 +59,7 @@
 def place_slots(slot, moved):
     number = lax.broadcasted_iota(jnp.int32, (PEERS * SLOTS, moved.shape[0]), 0)
     member = jnp.where(number == slot, 1.0, 0.0).astype(jnp.bfloat16)
-    high, low = halves(moved)
-    return dot(member, high) + dot(member, low)
+    return dot_exact(member, moved)
 
 
 def inner_kernel(
@@ -126,7 +129,7 @@
     loads[4].wait()
 
 
-def outer_kernel(pair_ref, cross_ref, high_ref, low_ref, edge_ref, edge_map_ref, slot_ref, label_ref, *rest):
+def outer_kernel(cross_ref, pair_ref, high_ref, low_ref, edge_ref, edge_map_ref, slot_ref, label_ref, *rest):
     *placed_refs, out_ref = rest
     taps = pair_ref.shape[1]
     parts = taps // LANES
@@ -180,8 +183,7 @@
         for k in (c, c + 1):
             starts = [peer * length + k * SLOTS for peer in range(PEERS)]
             pair.append(jnp.concatenate([arrived_ref[start : start + SLOTS, :] for start in starts], axis=0))
-        high, low = halves(jnp.concatenate(pair, axis=1))
-        total = dot(member, high) + dot(member, low)
+        total = dot_exact(member, jnp.concatenate(pair, axis=1))
         for k in (0, 1):
             for u in range(NU):
                 start = u * out_length + (c + k) * BIN_DEV
@@ -276,12 +278,13 @@
     taps = filters.shape[1]
     odd = lax.axis_index("section") % 2
     ends = [lax.dynamic_slice_in_dim(traces, (width - taps) * use_tail, taps, 1) for use_tail in (1 - odd, odd)]
-    pair, cross = swapped(ends[0], "section", 0), swapped(ends[1], "section", 1)
+    cross = swapped(ends[1], "section", 1)
+    pair = swapped(ends[0], "section", 0)
     code = (owners.reshape(1, rows) * BIN_DEV + sub_bins.reshape(1, rows)).astype(jnp.float32)
     small = jnp.pad(filters, ((0, 0), (0, taps + LANES))) + jnp.pad(code, ((0, 0), (2 * taps, LANES - rows)))
     kept = correct_inner(small, traces, sample_map)
     parts = width // LANES
-    sent = on_vmem(outer_kernel, (PEERS * (parts * SLOTS + 1), LANES), "correct_outer", pair, cross, *kept)
+    sent = on_vmem(outer_kernel, (PEERS * (parts * SLOTS + 1), LANES), "correct_outer", cross, pair, *kept)
     near = exchanged(sent, NEAR)
     summed = on_vmem(combine_kernel, (NU * (parts * BIN_DEV + 1), LANES), "combine", near)
     arrived = exchanged(summed, "u")

time: 71.3 us -> 71.9 us (level)
  the two profiles are of different devices: /device:TPU:6 before, /device:TPU:2 now
where the time goes in v6:
time: 71.9 us; the launch traced here: 71.6 us
  blocking collectives  54.5 us (76%)
  starting transfers between devices  9.74 us (14%)
  Pallas kernels  4.63 us (6%)
  other arithmetic  1.36 us (2%)
  local copies, waits for them, and re-layouts  0.88 us (1%)
    all_to_all x2, blocking collectives, exchanged(): lax.all_to_all(sent, axes, split_axis=0, concat_axis=0, tiled=True)  54.5 us
    ppermute x2, starting transfers between devices, swapped(): lax.ppermute(value, axis, pairs + [(other, one) for one, other in pairs])  9.74 us
    pallas_call x1, Pallas kernels, correct_inner(): pl.pallas_call(inner_kernel, out_shape=(jax.ShapeDtypeStruct((taps, 2 * t...  2.41 us
    pallas_call x3, Pallas kernels, on_vmem(): pl.pallas_call(kernel, out_shape=f32(*shape), in_specs=[VMEM] * len(opera...  2.22 us
  transfers between devices with their start and end apart: 2, of which 1 were waited for; matrix products, arithmetic and copies ran while one was open for 2% of the time, Pallas kernels for 3%

profile of v6, /device:TPU:2, one launch (start us, length us, event | category | flops | bytes accessed | tf_op | source)
XLA Modules:
  0.0 71.6 jit_solution(5470167808879560840)
XLA Ops:
  0.0 0.9 %constant_dynamic-slice_fusion = (f32[64,256]{1,0:T(8,128)S(1)}, f32[64,256]{1,0:T(8,128)S(1)}) fusion(f32[64,1024]{1,0:T(8,128)} %traces_hbm.1, s32[]{:T(128)S(6)} %select_n.15, s32[]{:T(128)S(6)} %select_n.14), kind=kLoop, calls=%fused_computation.4 | loop fusion | bytes 262152 | tf_op jit(solution)/shard_map/dynamic_slice | solution.py:280
  0.9 7.8 %collective-permute-start.1 = (f32[64,256]{1,0:T(8,128)S(1)}, f32[64,256]{1,0:T(8,128)S(1)}, u32[]{:S(2)}, u32[]{:S(2)}) collective-permute-start(f32[64,256]{1,0:T(8,128)S(1)} %get-tuple-element.25), channel_id=1, source_target_pairs={{0,128},{256,384},{128,0},{384,256},{1,129},{257,385},{129,1},{385... | collective-permute-start | bytes 196616 | tf_op jit(solution)/shard_map/ppermute | solution.py:267
  8.7 1.9 %collective-permute-start = (f32[64,256]{1,0:T(8,128)S(1)}, f32[64,256]{1,0:T(8,128)S(1)}, u32[]{:S(2)}, u32[]{:S(2)}) collective-permute-start(f32[64,256]{1,0:T(8,128)S(1)} %get-tuple-element.26), channel_id=1, source_target_pairs={{128,256},{256,128},{129,257},{257,129},{130,258},{258,130},{131,2... | collective-permute-start | bytes 196616 | tf_op jit(solution)/shard_map/ppermute | solution.py:267
  10.6 0.7 fusion.1
  11.3 0.7 pad_add_fusion.small_ref
  12.0 2.4 %correct_inner.1 = (bf16[256,512]{1,0:T(8,128)(2,1)S(1)}, bf16[256,512]{1,0:T(8,128)(2,1)S(1)}, f32[64,1024]{1,0:T(8,128)S(1)}, s32[64,512]{1,0:T(8,128)S(1)}, s...) custom-call(f32[1,640]{1,0:T(1,128)S(1)} %pad_add_fusion.small_ref, ...), custom_call_target="tpu_custom_call" | custom-call | flops 500000000 | bytes 2000000 | tf_op jit(solution)/shard_map/correct_inner/pallas_call | solution.py:229
  14.4 0.0 collective-permute-done.1.pair_ref
  14.4 0.4 collective-permute-done.cross_ref
  14.9 1.2 %correct_outer.1 = f32[2064,128]{1,0:T(8,128)S(1)} custom-call(f32[64,256]{1,0:T(8,128)S(1)} %collective-permute-done.cross_ref, f32[64,256]{1,0:T(8,128)S(1)} %collective-permute-done.1.pair_ref, bf16[256,512]{1,0:T(8,128)(2,1)S(1)} %get-tuple-element.15.high_ref, bf16[256,512]{1,0:T(8,128)(2,1)S(1)} %get-tuple-element.16.low_ref, ...), custom_call_target="tpu_custom_call" | custom-call | tf_op jit(solution)/shard_map/correct_outer/pallas_call | solution.py:254
  16.0 19.4 %all_to_all.10 = f32[2064,1,128]{2,1,0:T(1,128)S(1)} all-to-all(f32[2064,1,128]{2,1,0:T(1,128)S(1)} %bitcast.16), channel_id=1, replica_groups=mesh['section'=4,'y'=4,'u'=8,'w'=2,'c'=2] {'y','w','c'}, dimensions={0} | all-to-all | bytes 2113536 | tf_op jit(solution)/shard_map/all_to_all | solution.py:273
  35.4 0.3 combine.1
  35.8 35.1 %all_to_all.11 = f32[520,1,128]{2,1,0:T(1,128)S(1)} all-to-all(f32[520,1,128]{2,1,0:T(1,128)S(1)} %bitcast.18), channel_id=1, replica_groups=mesh['section'=4,'y'=4,'u'=8,'w'=2,'c'=2] {'u'}, dimensions={0} | all-to-all | bytes 532480 | tf_op jit(solution)/shard_map/all_to_all | solution.py:273
  70.9 0.7 %finish.1 = f32[8,1024]{1,0:T(8,128)} custom-call(f32[520,128]{1,0:T(8,128)S(1)} %bitcast.19), custom_call_target="tpu_custom_call" | custom-call | tf_op jit(solution)/shard_map/finish/pallas_call | solution.py:254
Async XLA Ops:
  0.9 13.5 %collective-permute-start.1 = (f32[64,256]{1,0:T(8,128)S(1)}, f32[64,256]{1,0:T(8,128)S(1)}, u32[]{:S(2)}, u32[]{:S(2)}) collective-permute-start(f32[64,256]{1,0:T(8,128)S(1)} %get-tuple-element.25), channel_id=1, source_target_pairs={{0,128},{256,384},{128,0},{384,256},{1,129},{257,385},{129,1},{385... | collective-permute-start | bytes 196616 | tf_op jit(solution)/shard_map/ppermute | solution.py:267
  8.7 6.2 %collective-permute-start = (f32[64,256]{1,0:T(8,128)S(1)}, f32[64,256]{1,0:T(8,128)S(1)}, u32[]{:S(2)}, u32[]{:S(2)}) collective-permute-start(f32[64,256]{1,0:T(8,128)S(1)} %get-tuple-element.26), channel_id=1, source_target_pairs={{128,256},{256,128},{129,257},{257,129},{130,258},{258,130},{131,2... | collective-permute-start | bytes 196616 | tf_op jit(solution)/shard_map/ppermute | solution.py:267

commit v7 on v6

--- a/solution.py
+++ b/solution.py
@@ -129,9 +129,9 @@
     loads[4].wait()
 
 
-def outer_kernel(cross_ref, pair_ref, high_ref, low_ref, edge_ref, edge_map_ref, slot_ref, label_ref, *rest):
+def outer_kernel(before_ref, after_ref, high_ref, low_ref, edge_ref, edge_map_ref, slot_ref, label_ref, *rest):
     *placed_refs, out_ref = rest
-    taps = pair_ref.shape[1]
+    taps = before_ref.shape[1]
     parts = taps // LANES
     length = out_ref.shape[0] // PEERS
     slot = slot_ref[...]
@@ -148,12 +148,9 @@
             put(c + i, placed[:, i * LANES : (i + 1) * LANES])
 
     place = lax.axis_index("section")
-    odd = lax.rem(place, 2) == 1
-    pair, cross = pair_ref[...], cross_ref[...]
-    before, after = jnp.where(odd, pair, cross), jnp.where(odd, cross, pair)
-    early = dot_split(halves(before), (high_ref[:, taps:], low_ref[:, taps:])) + edge_ref[:, :taps]
+    early = dot_split(halves(before_ref[...]), (high_ref[:, taps:], low_ref[:, taps:])) + edge_ref[:, :taps]
     put_edge(0, 0, jnp.concatenate([early, edge_ref[:, taps : 2 * taps]], axis=1))
-    late = dot_split(halves(after), (high_ref[:, :taps], low_ref[:, :taps])) + edge_ref[:, 3 * taps :]
+    late = dot_split(halves(after_ref[...]), (high_ref[:, :taps], low_ref[:, :taps])) + edge_ref[:, 3 * taps :]
     late = jnp.where(place == lax.axis_size("section") - 1, 0.0, late)
     put_edge(parts + len(placed_refs), parts, jnp.concatenate([edge_ref[:, 2 * taps : 3 * taps], late], axis=1))
     for c, placed_ref in enumerate(placed_refs):
@@ -261,10 +258,10 @@
     )(*operands)
 
 
-def swapped(value, axis, first):
+def passed_along(value, axis, steps):
     count = lax.axis_size(axis)
-    pairs = [(one, one + 1) for one in range(first, count - 1, 2)]
-    return lax.ppermute(value, axis, pairs + [(other, one) for one, other in pairs])
+    leading, last = (max(0, -steps), min(count, count - steps))
+    return lax.ppermute(value, axis, [(source, source + steps) for source in range(leading, last)])
 
 
 def exchanged(rows, axes):
@@ -276,15 +273,13 @@
 def per_device(traces, filters, owners, sub_bins, sample_map):
     rows, width = traces.shape
     taps = filters.shape[1]
-    odd = lax.axis_index("section") % 2
-    ends = [lax.dynamic_slice_in_dim(traces, (width - taps) * use_tail, taps, 1) for use_tail in (1 - odd, odd)]
-    cross = swapped(ends[1], "section", 1)
-    pair = swapped(ends[0], "section", 0)
+    before = passed_along(traces[:, width - taps :], "section", 1)
+    after = passed_along(traces[:, :taps], "section", -1)
     code = (owners.reshape(1, rows) * BIN_DEV + sub_bins.reshape(1, rows)).astype(jnp.float32)
     small = jnp.pad(filters, ((0, 0), (0, taps + LANES))) + jnp.pad(code, ((0, 0), (2 * taps, LANES - rows)))
     kept = correct_inner(small, traces, sample_map)
     parts = width // LANES
-    sent = on_vmem(outer_kernel, (PEERS * (parts * SLOTS + 1), LANES), "correct_outer", cross, pair, *kept)
+    sent = on_vmem(outer_kernel, (PEERS * (parts * SLOTS + 1), LANES), "correct_outer", before, after, *kept)
     near = exchanged(sent, NEAR)
     summed = on_vmem(combine_kernel, (NU * (parts * BIN_DEV + 1), LANES), "combine", near)
     arrived = exchanged(summed, "u")

time: 71.9 us -> 71.2 us (level)
  the two profiles are of different devices: /device:TPU:2 before, /device:TPU:6 now
where the time goes in v7:
time: 71.2 us; the launch traced here: 70.2 us
  blocking collectives  58.2 us (82%)
  Pallas kernels  4.62 us (6%)
  starting transfers between devices  4.03 us (6%)
  other arithmetic  1.36 us (2%)
  waiting for transfers between devices  1.08 us (2%)
  local copies, waits for them, and re-layouts  0.88 us (1%)
    all_to_all x2, blocking collectives, exchanged(): lax.all_to_all(sent, axes, split_axis=0, concat_axis=0, tiled=True)  58.2 us
    ppermute x2, starting transfers between devices, passed_along(): lax.ppermute(value, axis, [(source, source + steps) for source in range(l...  4.03 us
    pallas_call x1, Pallas kernels, correct_inner(): pl.pallas_call(inner_kernel, out_shape=(jax.ShapeDtypeStruct((taps, 2 * t...  2.4 us
    pallas_call x3, Pallas kernels, on_vmem(): pl.pallas_call(kernel, out_shape=f32(*shape), in_specs=[VMEM] * len(opera...  2.22 us
  transfers between devices with their start and end apart: 2, of which 1 were waited for; matrix products, arithmetic and copies ran while one was open for 2% of the time, Pallas kernels for 3%

profile of v7, /device:TPU:6, one launch (start us, length us, event | category | flops | bytes accessed | tf_op | source)
XLA Modules:
  0.0 70.2 jit_solution(1216453297797787690)
XLA Ops:
  0.0 0.9 %fusion.2 = (f32[64,256]{1,0:T(8,128)S(1)}, f32[64,256]{1,0:T(8,128)S(1)}) fusion(f32[64,1024]{1,0:T(8,128)} %traces_hbm.1), kind=kLoop, calls=%fused_computation.4 | loop fusion | bytes 262144 | tf_op jit(solution)/shard_map/slice | solution.py:277
  0.9 2.7 %collective-permute-start.1 = (f32[64,256]{1,0:T(8,128)S(1)}, f32[64,256]{1,0:T(8,128)S(1)}, u32[]{:S(2)}, u32[]{:S(2)}) collective-permute-start(f32[64,256]{1,0:T(8,128)S(1)} %get-tuple-element.25), channel_id=1, source_target_pairs={{128,0},{256,128},{384,256},{129,1},{257,129},{385,257},{130,2},{2... | collective-permute-start | bytes 196616 | tf_op jit(solution)/shard_map/ppermute | solution.py:264
  3.6 1.3 %collective-permute-start = (f32[64,256]{1,0:T(8,128)S(1)}, f32[64,256]{1,0:T(8,128)S(1)}, u32[]{:S(2)}, u32[]{:S(2)}) collective-permute-start(f32[64,256]{1,0:T(8,128)S(1)} %get-tuple-element.26), channel_id=1, source_target_pairs={{0,128},{128,256},{256,384},{1,129},{129,257},{257,385},{2,130},{1... | collective-permute-start | bytes 196616 | tf_op jit(solution)/shard_map/ppermute | solution.py:264
  4.9 0.7 fusion.1
  5.6 0.7 pad_add_fusion.small_ref
  6.3 2.4 %correct_inner.1 = (bf16[256,512]{1,0:T(8,128)(2,1)S(1)}, bf16[256,512]{1,0:T(8,128)(2,1)S(1)}, f32[64,1024]{1,0:T(8,128)S(1)}, s32[64,512]{1,0:T(8,128)S(1)}, s...) custom-call(f32[1,640]{1,0:T(1,128)S(1)} %pad_add_fusion.small_ref, ...), custom_call_target="tpu_custom_call" | custom-call | flops 500000000 | bytes 2000000 | tf_op jit(solution)/shard_map/correct_inner/pallas_call | solution.py:226
  8.7 0.0 collective-permute-done.1.after_ref
  8.7 1.1 %collective-permute-done.before_ref = f32[64,256]{1,0:T(8,128)S(1)} collective-permute-done((f32[64,256]{1,0:T(8,128)S(1)}, f32[64,256]{1,0:T(8,128)S(1)}, u32[]{:S(2)}, u32[]{:S(2)}) %collective-permute-start) | collective-permute-done | bytes 65568 | tf_op jit(solution)/shard_map/ppermute | solution.py:264
  9.8 1.2 %correct_outer.1 = f32[2064,128]{1,0:T(8,128)S(1)} custom-call(f32[64,256]{1,0:T(8,128)S(1)} %collective-permute-done.before_ref, f32[64,256]{1,0:T(8,128)S(1)} %collective-permute-done.1.after_ref, bf16[256,512]{1,0:T(8,128)(2,1)S(1)} %get-tuple-element.15.high_ref, bf16[256,512]{1,0:T(8,128)(2,1)S(1)} %get-tuple-element.16.low_ref, ...), custom_call_target="tpu_custom_call" | custom-call | tf_op jit(solution)/shard_map/correct_outer/pallas_call | solution.py:251
  11.0 22.5 %all_to_all.10 = f32[2064,1,128]{2,1,0:T(1,128)S(1)} all-to-all(f32[2064,1,128]{2,1,0:T(1,128)S(1)} %bitcast.16), channel_id=1, replica_groups=mesh['section'=4,'y'=4,'u'=8,'w'=2,'c'=2] {'y','w','c'}, dimensions={0} | all-to-all | bytes 2113536 | tf_op jit(solution)/shard_map/all_to_all | solution.py:270
  33.5 0.3 combine.1
  33.8 35.7 %all_to_all.11 = f32[520,1,128]{2,1,0:T(1,128)S(1)} all-to-all(f32[520,1,128]{2,1,0:T(1,128)S(1)} %bitcast.18), channel_id=1, replica_groups=mesh['section'=4,'y'=4,'u'=8,'w'=2,'c'=2] {'u'}, dimensions={0} | all-to-all | bytes 532480 | tf_op jit(solution)/shard_map/all_to_all | solution.py:270
  69.5 0.7 %finish.1 = f32[8,1024]{1,0:T(8,128)} custom-call(f32[520,128]{1,0:T(8,128)S(1)} %bitcast.19), custom_call_target="tpu_custom_call" | custom-call | tf_op jit(solution)/shard_map/finish/pallas_call | solution.py:251
Async XLA Ops:
  0.9 7.8 %collective-permute-start.1 = (f32[64,256]{1,0:T(8,128)S(1)}, f32[64,256]{1,0:T(8,128)S(1)}, u32[]{:S(2)}, u32[]{:S(2)}) collective-permute-start(f32[64,256]{1,0:T(8,128)S(1)} %get-tuple-element.25), channel_id=1, source_target_pairs={{128,0},{256,128},{384,256},{129,1},{257,129},{385,257},{130,2},{2... | collective-permute-start | bytes 196616 | tf_op jit(solution)/shard_map/ppermute | solution.py:264
  3.6 6.2 %collective-permute-start = (f32[64,256]{1,0:T(8,128)S(1)}, f32[64,256]{1,0:T(8,128)S(1)}, u32[]{:S(2)}, u32[]{:S(2)}) collective-permute-start(f32[64,256]{1,0:T(8,128)S(1)} %get-tuple-element.26), channel_id=1, source_target_pairs={{0,128},{128,256},{256,384},{1,129},{129,257},{257,385},{2,130},{1... | collective-permute-start | bytes 196616 | tf_op jit(solution)/shard_map/ppermute | solution.py:264

commit v8 on v7

--- a/solution.py
+++ b/solution.py
@@ -275,8 +275,9 @@
     taps = filters.shape[1]
     before = passed_along(traces[:, width - taps :], "section", 1)
     after = passed_along(traces[:, :taps], "section", -1)
-    code = (owners.reshape(1, rows) * BIN_DEV + sub_bins.reshape(1, rows)).astype(jnp.float32)
-    small = jnp.pad(filters, ((0, 0), (0, taps + LANES))) + jnp.pad(code, ((0, 0), (2 * taps, LANES - rows)))
+    around = ((0, 0), (2 * taps, LANES - rows))
+    owner, sub = jnp.pad(owners.reshape(1, rows), around), jnp.pad(sub_bins.reshape(1, rows), around)
+    small = jnp.pad(filters, ((0, 0), (0, taps + LANES))) + (owner * BIN_DEV + sub).astype(jnp.float32)
     kept = correct_inner(small, traces, sample_map)
     parts = width // LANES
     sent = on_vmem(outer_kernel, (PEERS * (parts * SLOTS + 1), LANES), "correct_outer", before, after, *kept)

time: 71.2 us -> 70.6 us (level)
  transfers between devices with their start and end apart: 2 -> 2, of which waited for: 1 -> 1; matrix products, arithmetic and copies ran while one was open for 2% -> 1% of each run, Pallas kernels for 3% -> 3%
where the time goes in v8:
time: 70.6 us; the launch traced here: 70.2 us
  blocking collectives  58.2 us (82%)
  Pallas kernels  4.62 us (7%)
  starting transfers between devices  4.03 us (6%)
  waiting for transfers between devices  1.72 us (2%)
  local copies, waits for them, and re-layouts  0.88 us (1%)
  other arithmetic  0.72 us (1%)
    all_to_all x2, blocking collectives, exchanged(): lax.all_to_all(sent, axes, split_axis=0, concat_axis=0, tiled=True)  58.2 us
    ppermute x2, starting transfers between devices, passed_along(): lax.ppermute(value, axis, [(source, source + steps) for source in range(l...  4.03 us
    pallas_call x1, Pallas kernels, correct_inner(): pl.pallas_call(inner_kernel, out_shape=(jax.ShapeDtypeStruct((taps, 2 * t...  2.4 us
    pallas_call x3, Pallas kernels, on_vmem(): pl.pallas_call(kernel, out_shape=f32(*shape), in_specs=[VMEM] * len(opera...  2.22 us
    ppermute x2, waiting for transfers between devices, passed_along(): lax.ppermute(value, axis, [(source, source + steps) for source in range(l...  1.72 us
  transfers between devices with their start and end apart: 2, of which 1 were waited for; matrix products, arithmetic and copies ran while one was open for 1% of the time, Pallas kernels for 3%

profile of v8, /device:TPU:6, one launch (start us, length us, event | category | flops | bytes accessed | tf_op | source)
XLA Modules:
  0.0 70.2 jit_solution(2888601325103536950)
XLA Ops:
  0.0 0.9 %fusion = (f32[64,256]{1,0:T(8,128)S(1)}, f32[64,256]{1,0:T(8,128)S(1)}) fusion(f32[64,1024]{1,0:T(8,128)} %traces_hbm.1), kind=kLoop, calls=%fused_computation.1 | loop fusion | bytes 262144 | tf_op jit(solution)/shard_map/slice | solution.py:277
  0.9 2.7 %collective-permute-start.1 = (f32[64,256]{1,0:T(8,128)S(1)}, f32[64,256]{1,0:T(8,128)S(1)}, u32[]{:S(2)}, u32[]{:S(2)}) collective-permute-start(f32[64,256]{1,0:T(8,128)S(1)} %get-tuple-element.25), channel_id=1, source_target_pairs={{128,0},{256,128},{384,256},{129,1},{257,129},{385,257},{130,2},{2... | collective-permute-start | bytes 196616 | tf_op jit(solution)/shard_map/ppermute | solution.py:264
  3.6 1.3 %collective-permute-start = (f32[64,256]{1,0:T(8,128)S(1)}, f32[64,256]{1,0:T(8,128)S(1)}, u32[]{:S(2)}, u32[]{:S(2)}) collective-permute-start(f32[64,256]{1,0:T(8,128)S(1)} %get-tuple-element.26), channel_id=1, source_target_pairs={{0,128},{128,256},{256,384},{1,129},{129,257},{257,385},{2,130},{1... | collective-permute-start | bytes 196616 | tf_op jit(solution)/shard_map/ppermute | solution.py:264
  4.9 0.7 %convert_add_fusion.small_ref = f32[1,640]{1,0:T(1,128)S(1)} fusion(s32[1,64]{1,0:T(1,128)} %bitcast.14, s32[1,64]{1,0:T(1,128)} %bitcast.15, f32[1,256]{1,0:T(1,128)} %param.6), kind=kLoop, calls=%fused_computation | loop fusion | flops 2560 | bytes 4096 | tf_op jit(solution)/shard_map/add | solution.py:280
  5.7 2.4 %correct_inner.1 = (bf16[256,512]{1,0:T(8,128)(2,1)S(1)}, bf16[256,512]{1,0:T(8,128)(2,1)S(1)}, f32[64,1024]{1,0:T(8,128)S(1)}, s32[64,512]{1,0:T(8,128)S(1)}, s...) custom-call(f32[1,640]{1,0:T(1,128)S(1)} %convert_add_fusion.small_r, ...), custom_call_target="tpu_custom_call" | custom-call | flops 500000000 | bytes 2000000 | tf_op jit(solution)/shard_map/correct_inner/pallas_call | solution.py:226
  8.1 0.0 collective-permute-done.1.after_ref
  8.1 1.7 %collective-permute-done.before_ref = f32[64,256]{1,0:T(8,128)S(1)} collective-permute-done((f32[64,256]{1,0:T(8,128)S(1)}, f32[64,256]{1,0:T(8,128)S(1)}, u32[]{:S(2)}, u32[]{:S(2)}) %collective-permute-start) | collective-permute-done | bytes 65568 | tf_op jit(solution)/shard_map/ppermute | solution.py:264
  9.8 1.2 %correct_outer.1 = f32[2064,128]{1,0:T(8,128)S(1)} custom-call(f32[64,256]{1,0:T(8,128)S(1)} %collective-permute-done.before_ref, f32[64,256]{1,0:T(8,128)S(1)} %collective-permute-done.1.after_ref, bf16[256,512]{1,0:T(8,128)(2,1)S(1)} %get-tuple-element.15.high_ref, bf16[256,512]{1,0:T(8,128)(2,1)S(1)} %get-tuple-element.16.low_ref, ...), custom_call_target="tpu_custom_call" | custom-call | tf_op jit(solution)/shard_map/correct_outer/pallas_call | solution.py:251
  11.0 22.5 %all_to_all.10 = f32[2064,1,128]{2,1,0:T(1,128)S(1)} all-to-all(f32[2064,1,128]{2,1,0:T(1,128)S(1)} %bitcast.10), channel_id=1, replica_groups=mesh['section'=4,'y'=4,'u'=8,'w'=2,'c'=2] {'y','w','c'}, dimensions={0} | all-to-all | bytes 2113536 | tf_op jit(solution)/shard_map/all_to_all | solution.py:270
  33.5 0.3 combine.1
  33.8 35.7 %all_to_all.11 = f32[520,1,128]{2,1,0:T(1,128)S(1)} all-to-all(f32[520,1,128]{2,1,0:T(1,128)S(1)} %bitcast.12), channel_id=1, replica_groups=mesh['section'=4,'y'=4,'u'=8,'w'=2,'c'=2] {'u'}, dimensions={0} | all-to-all | bytes 532480 | tf_op jit(solution)/shard_map/all_to_all | solution.py:270
  69.5 0.7 %finish.1 = f32[8,1024]{1,0:T(8,128)} custom-call(f32[520,128]{1,0:T(8,128)S(1)} %bitcast.13), custom_call_target="tpu_custom_call" | custom-call | tf_op jit(solution)/shard_map/finish/pallas_call | solution.py:251
Async XLA Ops:
  0.9 7.2 %collective-permute-start.1 = (f32[64,256]{1,0:T(8,128)S(1)}, f32[64,256]{1,0:T(8,128)S(1)}, u32[]{:S(2)}, u32[]{:S(2)}) collective-permute-start(f32[64,256]{1,0:T(8,128)S(1)} %get-tuple-element.25), channel_id=1, source_target_pairs={{128,0},{256,128},{384,256},{129,1},{257,129},{385,257},{130,2},{2... | collective-permute-start | bytes 196616 | tf_op jit(solution)/shard_map/ppermute | solution.py:264
  3.6 6.2 %collective-permute-start = (f32[64,256]{1,0:T(8,128)S(1)}, f32[64,256]{1,0:T(8,128)S(1)}, u32[]{:S(2)}, u32[]{:S(2)}) collective-permute-start(f32[64,256]{1,0:T(8,128)S(1)} %get-tuple-element.26), channel_id=1, source_target_pairs={{0,128},{128,256},{256,384},{1,129},{129,257},{257,385},{2,130},{1... | collective-permute-start | bytes 196616 | tf_op jit(solution)/shard_map/ppermute | solution.py:264

commit v9 on v8

--- a/solution.py
+++ b/solution.py
@@ -141,18 +141,18 @@
             start = peer * length + c * SLOTS
             out_ref[start : start + SLOTS, :] = placed[peer * SLOTS : (peer + 1) * SLOTS, :]
 
-    def put_edge(c, k, window):
-        quarters = [edge_map_ref[:, (k + i) * LANES : (k + i + 1) * LANES] for i in range(parts)]
-        placed = place_slots(slot, move_out(window, quarters))
-        for i in range(parts):
-            put(c + i, placed[:, i * LANES : (i + 1) * LANES])
-
-    place = lax.axis_index("section")
+    def moved(k, window):
+        return move_out(window, [edge_map_ref[:, (k + i) * LANES : (k + i + 1) * LANES] for i in range(parts)])
+
     early = dot_split(halves(before_ref[...]), (high_ref[:, taps:], low_ref[:, taps:])) + edge_ref[:, :taps]
-    put_edge(0, 0, jnp.concatenate([early, edge_ref[:, taps : 2 * taps]], axis=1))
     late = dot_split(halves(after_ref[...]), (high_ref[:, :taps], low_ref[:, :taps])) + edge_ref[:, 3 * taps :]
-    late = jnp.where(place == lax.axis_size("section") - 1, 0.0, late)
-    put_edge(parts + len(placed_refs), parts, jnp.concatenate([edge_ref[:, 2 * taps : 3 * taps], late], axis=1))
+    late = jnp.where(lax.axis_index("section") == lax.axis_size("section") - 1, 0.0, late)
+    first = moved(0, jnp.concatenate([early, edge_ref[:, taps : 2 * taps]], axis=1))
+    last = moved(parts, jnp.concatenate([edge_ref[:, 2 * taps : 3 * taps], late], axis=1))
+    placed = place_slots(slot, jnp.concatenate([first, last], axis=1))
+    places = [*range(parts), *range(parts + len(placed_refs), 2 * parts + len(placed_refs))]
+    for i, c in enumerate(places):
+        put(c, placed[:, i * LANES : (i + 1) * LANES])
     for c, placed_ref in enumerate(placed_refs):
         put(parts + c, placed_ref)
     for peer in range(PEERS):

time: 70.6 us -> 70.4 us (level)
  no operation moved by 1% of the time
where the time goes in v9:
time: 70.4 us; the launch traced here: 70 us
  blocking collectives  58.2 us (83%)
  Pallas kernels  4.42 us (6%)
  starting transfers between devices  4.03 us (6%)
  waiting for transfers between devices  1.72 us (2%)
  local copies, waits for them, and re-layouts  0.88 us (1%)
  other arithmetic  0.72 us (1%)
    all_to_all x2, blocking collectives, exchanged(): lax.all_to_all(sent, axes, split_axis=0, concat_axis=0, tiled=True)  58.2 us
    ppermute x2, starting transfers between devices, passed_along(): lax.ppermute(value, axis, [(source, source + steps) for source in range(l...  4.03 us
    pallas_call x1, Pallas kernels, correct_inner(): pl.pallas_call(inner_kernel, out_shape=(jax.ShapeDtypeStruct((taps, 2 * t...  2.4 us
    pallas_call x3, Pallas kernels, on_vmem(): pl.pallas_call(kernel, out_shape=f32(*shape), in_specs=[VMEM] * len(opera...  2.02 us
    ppermute x2, waiting for transfers between devices, passed_along(): lax.ppermute(value, axis, [(source, source + steps) for source in range(l...  1.72 us
  transfers between devices with their start and end apart: 2, of which 1 were waited for; matrix products, arithmetic and copies ran while one was open for 1% of the time, Pallas kernels for 3%

profile of v9, /device:TPU:6, one launch (start us, length us, event | category | flops | bytes accessed | tf_op | source)
XLA Modules:
  0.0 70.0 jit_solution(16967783090521972712)
XLA Ops:
  0.0 0.9 %fusion = (f32[64,256]{1,0:T(8,128)S(1)}, f32[64,256]{1,0:T(8,128)S(1)}) fusion(f32[64,1024]{1,0:T(8,128)} %traces_hbm.1), kind=kLoop, calls=%fused_computation.1 | loop fusion | bytes 262144 | tf_op jit(solution)/shard_map/slice | solution.py:277
  0.9 2.7 %collective-permute-start.1 = (f32[64,256]{1,0:T(8,128)S(1)}, f32[64,256]{1,0:T(8,128)S(1)}, u32[]{:S(2)}, u32[]{:S(2)}) collective-permute-start(f32[64,256]{1,0:T(8,128)S(1)} %get-tuple-element.25), channel_id=1, source_target_pairs={{128,0},{256,128},{384,256},{129,1},{257,129},{385,257},{130,2},{2... | collective-permute-start | bytes 196616 | tf_op jit(solution)/shard_map/ppermute | solution.py:264
  3.6 1.3 %collective-permute-start = (f32[64,256]{1,0:T(8,128)S(1)}, f32[64,256]{1,0:T(8,128)S(1)}, u32[]{:S(2)}, u32[]{:S(2)}) collective-permute-start(f32[64,256]{1,0:T(8,128)S(1)} %get-tuple-element.26), channel_id=1, source_target_pairs={{0,128},{128,256},{256,384},{1,129},{129,257},{257,385},{2,130},{1... | collective-permute-start | bytes 196616 | tf_op jit(solution)/shard_map/ppermute | solution.py:264
  4.9 0.7 %convert_add_fusion.small_ref = f32[1,640]{1,0:T(1,128)S(1)} fusion(s32[1,64]{1,0:T(1,128)} %bitcast.14, s32[1,64]{1,0:T(1,128)} %bitcast.15, f32[1,256]{1,0:T(1,128)} %param.6), kind=kLoop, calls=%fused_computation | loop fusion | flops 2560 | bytes 4096 | tf_op jit(solution)/shard_map/add | solution.py:280
  5.7 2.4 %correct_inner.1 = (bf16[256,512]{1,0:T(8,128)(2,1)S(1)}, bf16[256,512]{1,0:T(8,128)(2,1)S(1)}, f32[64,1024]{1,0:T(8,128)S(1)}, s32[64,512]{1,0:T(8,128)S(1)}, s...) custom-call(f32[1,640]{1,0:T(1,128)S(1)} %convert_add_fusion.small_r, ...), custom_call_target="tpu_custom_call" | custom-call | flops 500000000 | bytes 2000000 | tf_op jit(solution)/shard_map/correct_inner/pallas_call | solution.py:226
  8.1 0.0 collective-permute-done.1.after_ref
  8.1 1.7 %collective-permute-done.before_ref = f32[64,256]{1,0:T(8,128)S(1)} collective-permute-done((f32[64,256]{1,0:T(8,128)S(1)}, f32[64,256]{1,0:T(8,128)S(1)}, u32[]{:S(2)}, u32[]{:S(2)}) %collective-permute-start) | collective-permute-done | bytes 65568 | tf_op jit(solution)/shard_map/ppermute | solution.py:264
  9.8 1.0 %correct_outer.1 = f32[2064,128]{1,0:T(8,128)S(1)} custom-call(f32[64,256]{1,0:T(8,128)S(1)} %collective-permute-done.before_ref, f32[64,256]{1,0:T(8,128)S(1)} %collective-permute-done.1.after_ref, bf16[256,512]{1,0:T(8,128)(2,1)S(1)} %get-tuple-element.15.high_ref, bf16[256,512]{1,0:T(8,128)(2,1)S(1)} %get-tuple-element.16.low_ref, ...), custom_call_target="tpu_custom_call" | custom-call | tf_op jit(solution)/shard_map/correct_outer/pallas_call | solution.py:251
  10.8 22.5 %all_to_all.10 = f32[2064,1,128]{2,1,0:T(1,128)S(1)} all-to-all(f32[2064,1,128]{2,1,0:T(1,128)S(1)} %bitcast.10), channel_id=1, replica_groups=mesh['section'=4,'y'=4,'u'=8,'w'=2,'c'=2] {'y','w','c'}, dimensions={0} | all-to-all | bytes 2113536 | tf_op jit(solution)/shard_map/all_to_all | solution.py:270
  33.3 0.3 combine.1
  33.6 35.7 %all_to_all.11 = f32[520,1,128]{2,1,0:T(1,128)S(1)} all-to-all(f32[520,1,128]{2,1,0:T(1,128)S(1)} %bitcast.12), channel_id=1, replica_groups=mesh['section'=4,'y'=4,'u'=8,'w'=2,'c'=2] {'u'}, dimensions={0} | all-to-all | bytes 532480 | tf_op jit(solution)/shard_map/all_to_all | solution.py:270
  69.3 0.7 %finish.1 = f32[8,1024]{1,0:T(8,128)} custom-call(f32[520,128]{1,0:T(8,128)S(1)} %bitcast.13), custom_call_target="tpu_custom_call" | custom-call | tf_op jit(solution)/shard_map/finish/pallas_call | solution.py:251
Async XLA Ops:
  0.9 7.2 %collective-permute-start.1 = (f32[64,256]{1,0:T(8,128)S(1)}, f32[64,256]{1,0:T(8,128)S(1)}, u32[]{:S(2)}, u32[]{:S(2)}) collective-permute-start(f32[64,256]{1,0:T(8,128)S(1)} %get-tuple-element.25), channel_id=1, source_target_pairs={{128,0},{256,128},{384,256},{129,1},{257,129},{385,257},{130,2},{2... | collective-permute-start | bytes 196616 | tf_op jit(solution)/shard_map/ppermute | solution.py:264
  3.6 6.2 %collective-permute-start = (f32[64,256]{1,0:T(8,128)S(1)}, f32[64,256]{1,0:T(8,128)S(1)}, u32[]{:S(2)}, u32[]{:S(2)}) collective-permute-start(f32[64,256]{1,0:T(8,128)S(1)} %get-tuple-element.26), channel_id=1, source_target_pairs={{0,128},{128,256},{256,384},{1,129},{129,257},{257,385},{2,130},{1... | collective-permute-start | bytes 196616 | tf_op jit(solution)/shard_map/ppermute | solution.py:264

commit v10 on v9

--- a/solution.py
+++ b/solution.py
@@ -73,8 +73,8 @@
     count = width // taps
     loads = []
     for part in range(2):
-        columns = pl.ds(part * half, half)
-        loads.append(pltpu.make_async_copy(traces_hbm.at[:, columns], traces_ref.at[:, columns], sems.at[part]))
+        some = pl.ds(part * (rows // 2), rows // 2)
+        loads.append(pltpu.make_async_copy(traces_hbm.at[some, :], traces_ref.at[some, :], sems.at[part]))
     loads += [
         pltpu.make_async_copy(map_hbm.at[:, taps : taps + half], map_ref, sems.at[2]),
         pltpu.make_async_copy(map_hbm.at[:, :taps], edge_map_ref.at[:, :taps], sems.at[3]),

time: 70.4 us -> 70.4 us (level)
  no operation moved by 1% of the time
where the time goes in v10:
time: 70.4 us; the launch traced here: 70 us
  blocking collectives  58.2 us (83%)
  Pallas kernels  4.37 us (6%)
  starting transfers between devices  4.03 us (6%)
  waiting for transfers between devices  1.77 us (3%)
  local copies, waits for them, and re-layouts  0.88 us (1%)
  other arithmetic  0.72 us (1%)
    all_to_all x2, blocking collectives, exchanged(): lax.all_to_all(sent, axes, split_axis=0, concat_axis=0, tiled=True)  58.2 us
    ppermute x2, starting transfers between devices, passed_along(): lax.ppermute(value, axis, [(source, source + steps) for source in range(l...  4.03 us
    pallas_call x1, Pallas kernels, correct_inner(): pl.pallas_call(inner_kernel, out_shape=(jax.ShapeDtypeStruct((taps, 2 * t...  2.35 us
    pallas_call x3, Pallas kernels, on_vmem(): pl.pallas_call(kernel, out_shape=f32(*shape), in_specs=[VMEM] * len(opera...  2.02 us
    ppermute x2, waiting for transfers between devices, passed_along(): lax.ppermute(value, axis, [(source, source + steps) for source in range(l...  1.77 us
  transfers between devices with their start and end apart: 2, of which 1 were waited for; matrix products, arithmetic and copies ran while one was open for 1% of the time, Pallas kernels for 3%

profile of v10, /device:TPU:6, one launch (start us, length us, event | category | flops | bytes accessed | tf_op | source)
XLA Modules:
  0.0 70.0 jit_solution(4812397372198615422)
XLA Ops:
  0.0 0.9 %fusion = (f32[64,256]{1,0:T(8,128)S(1)}, f32[64,256]{1,0:T(8,128)S(1)}) fusion(f32[64,1024]{1,0:T(8,128)} %traces_hbm.1), kind=kLoop, calls=%fused_computation.1 | loop fusion | bytes 262144 | tf_op jit(solution)/shard_map/slice | solution.py:277
  0.9 2.7 %collective-permute-start.1 = (f32[64,256]{1,0:T(8,128)S(1)}, f32[64,256]{1,0:T(8,128)S(1)}, u32[]{:S(2)}, u32[]{:S(2)}) collective-permute-start(f32[64,256]{1,0:T(8,128)S(1)} %get-tuple-element.25), channel_id=1, source_target_pairs={{128,0},{256,128},{384,256},{129,1},{257,129},{385,257},{130,2},{2... | collective-permute-start | bytes 196616 | tf_op jit(solution)/shard_map/ppermute | solution.py:264
  3.6 1.3 %collective-permute-start = (f32[64,256]{1,0:T(8,128)S(1)}, f32[64,256]{1,0:T(8,128)S(1)}, u32[]{:S(2)}, u32[]{:S(2)}) collective-permute-start(f32[64,256]{1,0:T(8,128)S(1)} %get-tuple-element.26), channel_id=1, source_target_pairs={{0,128},{128,256},{256,384},{1,129},{129,257},{257,385},{2,130},{1... | collective-permute-start | bytes 196616 | tf_op jit(solution)/shard_map/ppermute | solution.py:264
  4.9 0.7 %convert_add_fusion.small_ref = f32[1,640]{1,0:T(1,128)S(1)} fusion(s32[1,64]{1,0:T(1,128)} %bitcast.14, s32[1,64]{1,0:T(1,128)} %bitcast.15, f32[1,256]{1,0:T(1,128)} %param.6), kind=kLoop, calls=%fused_computation | loop fusion | flops 2560 | bytes 4096 | tf_op jit(solution)/shard_map/add | solution.py:280
  5.7 2.4 %correct_inner.1 = (bf16[256,512]{1,0:T(8,128)(2,1)S(1)}, bf16[256,512]{1,0:T(8,128)(2,1)S(1)}, f32[64,1024]{1,0:T(8,128)S(1)}, s32[64,512]{1,0:T(8,128)S(1)}, s...) custom-call(f32[1,640]{1,0:T(1,128)S(1)} %convert_add_fusion.small_r, ...), custom_call_target="tpu_custom_call" | custom-call | flops 500000000 | bytes 2000000 | tf_op jit(solution)/shard_map/correct_inner/pallas_call | solution.py:226
  8.0 0.0 collective-permute-done.1.after_ref
  8.0 1.8 %collective-permute-done.before_ref = f32[64,256]{1,0:T(8,128)S(1)} collective-permute-done((f32[64,256]{1,0:T(8,128)S(1)}, f32[64,256]{1,0:T(8,128)S(1)}, u32[]{:S(2)}, u32[]{:S(2)}) %collective-permute-start) | collective-permute-done | bytes 65568 | tf_op jit(solution)/shard_map/ppermute | solution.py:264
  9.8 1.0 %correct_outer.1 = f32[2064,128]{1,0:T(8,128)S(1)} custom-call(f32[64,256]{1,0:T(8,128)S(1)} %collective-permute-done.before_ref, f32[64,256]{1,0:T(8,128)S(1)} %collective-permute-done.1.after_ref, bf16[256,512]{1,0:T(8,128)(2,1)S(1)} %get-tuple-element.15.high_ref, bf16[256,512]{1,0:T(8,128)(2,1)S(1)} %get-tuple-element.16.low_ref, ...), custom_call_target="tpu_custom_call" | custom-call | tf_op jit(solution)/shard_map/correct_outer/pallas_call | solution.py:251
  10.8 22.5 %all_to_all.10 = f32[2064,1,128]{2,1,0:T(1,128)S(1)} all-to-all(f32[2064,1,128]{2,1,0:T(1,128)S(1)} %bitcast.10), channel_id=1, replica_groups=mesh['section'=4,'y'=4,'u'=8,'w'=2,'c'=2] {'y','w','c'}, dimensions={0} | all-to-all | bytes 2113536 | tf_op jit(solution)/shard_map/all_to_all | solution.py:270
  33.3 0.3 combine.1
  33.6 35.7 %all_to_all.11 = f32[520,1,128]{2,1,0:T(1,128)S(1)} all-to-all(f32[520,1,128]{2,1,0:T(1,128)S(1)} %bitcast.12), channel_id=1, replica_groups=mesh['section'=4,'y'=4,'u'=8,'w'=2,'c'=2] {'u'}, dimensions={0} | all-to-all | bytes 532480 | tf_op jit(solution)/shard_map/all_to_all | solution.py:270
  69.3 0.7 %finish.1 = f32[8,1024]{1,0:T(8,128)} custom-call(f32[520,128]{1,0:T(8,128)S(1)} %bitcast.13), custom_call_target="tpu_custom_call" | custom-call | tf_op jit(solution)/shard_map/finish/pallas_call | solution.py:251
Async XLA Ops:
  0.9 7.1 %collective-permute-start.1 = (f32[64,256]{1,0:T(8,128)S(1)}, f32[64,256]{1,0:T(8,128)S(1)}, u32[]{:S(2)}, u32[]{:S(2)}) collective-permute-start(f32[64,256]{1,0:T(8,128)S(1)} %get-tuple-element.25), channel_id=1, source_target_pairs={{128,0},{256,128},{384,256},{129,1},{257,129},{385,257},{130,2},{2... | collective-permute-start | bytes 196616 | tf_op jit(solution)/shard_map/ppermute | solution.py:264
  3.6 6.2 %collective-permute-start = (f32[64,256]{1,0:T(8,128)S(1)}, f32[64,256]{1,0:T(8,128)S(1)}, u32[]{:S(2)}, u32[]{:S(2)}) collective-permute-start(f32[64,256]{1,0:T(8,128)S(1)} %get-tuple-element.26), channel_id=1, source_target_pairs={{0,128},{128,256},{256,384},{1,129},{129,257},{257,385},{2,130},{1... | collective-permute-start | bytes 196616 | tf_op jit(solution)/shard_map/ppermute | solution.py:264

commit v11 on v10

--- a/solution.py
+++ b/solution.py
@@ -202,11 +202,11 @@
     fold = sum(arrived_ref[(u + 1) * length - 1 : (u + 1) * length, :] for u in range(NU))
     diagonal = lax.broadcasted_iota(jnp.int32, (BIN_DEV, LANES), 0) == lax.broadcasted_iota(jnp.int32, (BIN_DEV, LANES), 1)
     counts = jnp.sum(jnp.where(diagonal, fold, 0.0), axis=1, keepdims=True)
-    scale = jnp.sqrt(jnp.maximum(counts, 1.0))
+    scale = jnp.broadcast_to(1.0 / jnp.sqrt(jnp.maximum(counts, 1.0)), (BIN_DEV, LANES))
     for c in range(length // BIN_DEV):
         starts = [u * length + c * BIN_DEV for u in range(NU)]
         total = sum(arrived_ref[start : start + BIN_DEV, :] for start in starts)
-        out_ref[:, c * LANES : (c + 1) * LANES] = total / scale
+        out_ref[:, c * LANES : (c + 1) * LANES] = total * scale
 
 
 VMEM = pl.BlockSpec(memory_space=pltpu.VMEM)

time: 70.4 us -> 70.4 us (level)
  no operation moved by 1% of the time
where the time goes in v11:
time: 70.4 us; the launch traced here: 70 us
  blocking collectives  58.2 us (83%)
  Pallas kernels  4.37 us (6%)
  starting transfers between devices  4.03 us (6%)
  waiting for transfers between devices  1.77 us (3%)
  local copies, waits for them, and re-layouts  0.88 us (1%)
  other arithmetic  0.72 us (1%)
    all_to_all x2, blocking collectives, exchanged(): lax.all_to_all(sent, axes, split_axis=0, concat_axis=0, tiled=True)  58.2 us
    ppermute x2, starting transfers between devices, passed_along(): lax.ppermute(value, axis, [(source, source + steps) for source in range(l...  4.03 us
    pallas_call x1, Pallas kernels, correct_inner(): pl.pallas_call(inner_kernel, out_shape=(jax.ShapeDtypeStruct((taps, 2 * t...  2.35 us
    pallas_call x3, Pallas kernels, on_vmem(): pl.pallas_call(kernel, out_shape=f32(*shape), in_specs=[VMEM] * len(opera...  2.02 us
    ppermute x2, waiting for transfers between devices, passed_along(): lax.ppermute(value, axis, [(source, source + steps) for source in range(l...  1.77 us
  transfers between devices with their start and end apart: 2, of which 1 were waited for; matrix products, arithmetic and copies ran while one was open for 1% of the time, Pallas kernels for 3%

profile of v11, /device:TPU:6, one launch (start us, length us, event | category | flops | bytes accessed | tf_op | source)
XLA Modules:
  0.0 70.0 jit_solution(4812397372198615422)
XLA Ops:
  0.0 0.9 %fusion = (f32[64,256]{1,0:T(8,128)S(1)}, f32[64,256]{1,0:T(8,128)S(1)}) fusion(f32[64,1024]{1,0:T(8,128)} %traces_hbm.1), kind=kLoop, calls=%fused_computation.1 | loop fusion | bytes 262144 | tf_op jit(solution)/shard_map/slice | solution.py:277
  0.9 2.7 %collective-permute-start.1 = (f32[64,256]{1,0:T(8,128)S(1)}, f32[64,256]{1,0:T(8,128)S(1)}, u32[]{:S(2)}, u32[]{:S(2)}) collective-permute-start(f32[64,256]{1,0:T(8,128)S(1)} %get-tuple-element.25), channel_id=1, source_target_pairs={{128,0},{256,128},{384,256},{129,1},{257,129},{385,257},{130,2},{2... | collective-permute-start | bytes 196616 | tf_op jit(solution)/shard_map/ppermute | solution.py:264
  3.6 1.3 %collective-permute-start = (f32[64,256]{1,0:T(8,128)S(1)}, f32[64,256]{1,0:T(8,128)S(1)}, u32[]{:S(2)}, u32[]{:S(2)}) collective-permute-start(f32[64,256]{1,0:T(8,128)S(1)} %get-tuple-element.26), channel_id=1, source_target_pairs={{0,128},{128,256},{256,384},{1,129},{129,257},{257,385},{2,130},{1... | collective-permute-start | bytes 196616 | tf_op jit(solution)/shard_map/ppermute | solution.py:264
  4.9 0.7 %convert_add_fusion.small_ref = f32[1,640]{1,0:T(1,128)S(1)} fusion(s32[1,64]{1,0:T(1,128)} %bitcast.14, s32[1,64]{1,0:T(1,128)} %bitcast.15, f32[1,256]{1,0:T(1,128)} %param.6), kind=kLoop, calls=%fused_computation | loop fusion | flops 2560 | bytes 4096 | tf_op jit(solution)/shard_map/add | solution.py:280
  5.7 2.4 %correct_inner.1 = (bf16[256,512]{1,0:T(8,128)(2,1)S(1)}, bf16[256,512]{1,0:T(8,128)(2,1)S(1)}, f32[64,1024]{1,0:T(8,128)S(1)}, s32[64,512]{1,0:T(8,128)S(1)}, s...) custom-call(f32[1,640]{1,0:T(1,128)S(1)} %convert_add_fusion.small_r, ...), custom_call_target="tpu_custom_call" | custom-call | flops 500000000 | bytes 2000000 | tf_op jit(solution)/shard_map/correct_inner/pallas_call | solution.py:226
  8.0 0.0 collective-permute-done.1.after_ref
  8.0 1.8 %collective-permute-done.before_ref = f32[64,256]{1,0:T(8,128)S(1)} collective-permute-done((f32[64,256]{1,0:T(8,128)S(1)}, f32[64,256]{1,0:T(8,128)S(1)}, u32[]{:S(2)}, u32[]{:S(2)}) %collective-permute-start) | collective-permute-done | bytes 65568 | tf_op jit(solution)/shard_map/ppermute | solution.py:264
  9.8 1.0 %correct_outer.1 = f32[2064,128]{1,0:T(8,128)S(1)} custom-call(f32[64,256]{1,0:T(8,128)S(1)} %collective-permute-done.before_ref, f32[64,256]{1,0:T(8,128)S(1)} %collective-permute-done.1.after_ref, bf16[256,512]{1,0:T(8,128)(2,1)S(1)} %get-tuple-element.15.high_ref, bf16[256,512]{1,0:T(8,128)(2,1)S(1)} %get-tuple-element.16.low_ref, ...), custom_call_target="tpu_custom_call" | custom-call | tf_op jit(solution)/shard_map/correct_outer/pallas_call | solution.py:251
  10.8 22.5 %all_to_all.10 = f32[2064,1,128]{2,1,0:T(1,128)S(1)} all-to-all(f32[2064,1,128]{2,1,0:T(1,128)S(1)} %bitcast.10), channel_id=1, replica_groups=mesh['section'=4,'y'=4,'u'=8,'w'=2,'c'=2] {'y','w','c'}, dimensions={0} | all-to-all | bytes 2113536 | tf_op jit(solution)/shard_map/all_to_all | solution.py:270
  33.3 0.3 combine.1
  33.6 35.7 %all_to_all.11 = f32[520,1,128]{2,1,0:T(1,128)S(1)} all-to-all(f32[520,1,128]{2,1,0:T(1,128)S(1)} %bitcast.12), channel_id=1, replica_groups=mesh['section'=4,'y'=4,'u'=8,'w'=2,'c'=2] {'u'}, dimensions={0} | all-to-all | bytes 532480 | tf_op jit(solution)/shard_map/all_to_all | solution.py:270
  69.3 0.7 %finish.1 = f32[8,1024]{1,0:T(8,128)} custom-call(f32[520,128]{1,0:T(8,128)S(1)} %bitcast.13), custom_call_target="tpu_custom_call" | custom-call | tf_op jit(solution)/shard_map/finish/pallas_call | solution.py:251
Async XLA Ops:
  0.9 7.1 %collective-permute-start.1 = (f32[64,256]{1,0:T(8,128)S(1)}, f32[64,256]{1,0:T(8,128)S(1)}, u32[]{:S(2)}, u32[]{:S(2)}) collective-permute-start(f32[64,256]{1,0:T(8,128)S(1)} %get-tuple-element.25), channel_id=1, source_target_pairs={{128,0},{256,128},{384,256},{129,1},{257,129},{385,257},{130,2},{2... | collective-permute-start | bytes 196616 | tf_op jit(solution)/shard_map/ppermute | solution.py:264
  3.6 6.2 %collective-permute-start = (f32[64,256]{1,0:T(8,128)S(1)}, f32[64,256]{1,0:T(8,128)S(1)}, u32[]{:S(2)}, u32[]{:S(2)}) collective-permute-start(f32[64,256]{1,0:T(8,128)S(1)} %get-tuple-element.26), channel_id=1, source_target_pairs={{0,128},{128,256},{256,384},{1,129},{129,257},{257,385},{2,130},{1... | collective-permute-start | bytes 196616 | tf_op jit(solution)/shard_map/ppermute | solution.py:264
